TPU v7x, 32 devices: a whole 2x2x4 slice. The times are simulated.
32 devices in a mesh: groups: 1, cand: 32 (over z, y, x, core).
Axes of the slice: x: 2, y: 2, z: 4, core: 2. Of those that a mesh axis runs over, the one named last changes fastest.
Arguments:
- users: bfloat16 [128, 1024], P(('groups', 'cand')), may hold values from -6 to 6
- items: bfloat16 [32768, 1024], P(('groups', 'cand')), may hold values from -6 to 6
- probes: int32 [128, 32], P(('groups', 'cand')), may hold values from 0 to 63, all different within a row; in each aligned block of 4 rows (0 to 3, 4 to 7, ...) at most 4 rows name the same one
- gate_weight: bfloat16 [64, 64], replicated, may hold values from -0.75 to 0.75
- gate_bias: float32 [64], replicated, may hold values from -2 to 2
- cross_weight: bfloat16 [3, 1024, 1024], replicated, may hold values from -0.09375 to 0.09375
- cross_bias: float32 [3, 1024], replicated, may hold values from -0.5 to 0.5
- out_weight: float32 [1024], replicated, may hold values from -0.1875 to 0.1875
- row_device: int32 [24576, 1], P(('groups', 'cand')), may hold values from 0 to 31; in each aligned block of 768 rows (0 to 767, 768 to 1535, ...) at most 48 rows name the same one
- row_item: int32 [24576], P(('groups', 'cand')), may hold values from 0 to 1023
- row_request: int32 [24576], P(('groups', 'cand')), may hold values from 0 to 127
Outputs:
- top_scores: float32 [128, 96], P(('groups', 'cand'))
- rerank: float32 [24576], P(('groups', 'cand'))
Inputs may be any that keep to these rules, and one draw needn't show every extreme that they name: `probes`: each row names 32 different clusters. Among the requests of one index of cand, no cluster is named by more than 4 of them, a bound that some block reaches. `row_device`: among the rows of one index of cand, no index is named more than 48 times, a bound that some block reaches.
All inputs are finite; a program needn't handle non-finite values.
Results may differ from a plain program's by a relative error of at most 0.0037.
Values may be sent and summed in bfloat16 or wider, within the bound.
No kernel may reach another device: no remote copies, remote signals or barrier semaphores. Data moves between devices by JAX's collectives and lax.ppermute only.
A program may use at most 128 MiB of HBM per device.

v0:
```python
import functools
import math

import jax
import jax.numpy as jnp
from jax import lax
from jax.experimental import pallas as pl
from jax.experimental.pallas import tpu as pltpu
from jax.sharding import PartitionSpec as P

EMB = 8
D = 128
PAIRS = EMB * EMB
PROBES = 32
KEEP = 96
CL_DEV = 2
REQ_DEV = 4
LANES = 128
TILE_COLS = 256
GROUP = 4
BASE = 32
LOG2E = math.log2(math.e)
SCALE = 1.0 / math.sqrt(D)
VMEM = 56 * 1024 * 1024

F32 = jnp.float32
BF16 = jnp.bfloat16
NT = (((1,), (1,)), ((), ()))


def iota(shape, dim):
    return lax.broadcasted_iota(jnp.int32, shape, dim)


def dot(a, b):
    return jnp.dot(a, b, preferred_element_type=F32)


def dot_nt(a, b):
    return lax.dot_general(a, b, NT, preferred_element_type=F32)


def ones_where(cond):
    return jnp.where(cond, 1.0, 0.0).astype(BF16)


def split_two(x):
    high = x.astype(BF16)
    return high, (x - high.astype(F32)).astype(BF16)


def plan_kernel(owner_ref, item_ref, request_ref, probes_ref, gate_ref, bias_ref,
                codes_ref, place_ref, gate_out, bias_out):
    rows = owner_ref.shape[1]
    size = codes_ref.shape[0]
    at = owner_ref[...] == iota((size, rows), 0)
    at_one = ones_where(at)
    before = ones_where(iota((rows, rows), 0) < iota((rows, rows), 1))
    rank = dot(at_one, before)
    place = jnp.sum(jnp.where(at, rank, 0.0), axis=0, keepdims=True).astype(jnp.int32)
    place_ref[...] = place
    slots = ones_where(place == iota((LANES, rows), 0))
    item = item_ref[...]
    values = (item // BASE, item % BASE, request_ref[...])
    spread = jnp.concatenate(
        [jnp.where(at, value.astype(F32), 0.0).astype(BF16) for value in values], axis=0
    )
    codes = dot_nt(spread, slots)
    codes_ref[:, :LANES] = (codes[:size] * BASE + codes[size : 2 * size]).astype(jnp.int32)
    codes_ref[:, LANES : 2 * LANES] = codes[2 * size :].astype(jnp.int32)
    requests, probes = probes_ref.shape
    lane = iota((size, LANES), 1)
    masks = jnp.zeros((size, LANES), F32)
    for cluster in range(CL_DEV):
        ids = iota((size, probes), 0) * CL_DEV + cluster
        for request in range(requests):
            hit = jnp.where(probes_ref[request : request + 1, :] == ids, 1.0, 0.0)
            any_hit = jnp.max(hit, axis=1, keepdims=True)
            masks = jnp.where(lane == cluster * requests + request, any_hit, masks)
    codes_ref[:, 2 * LANES :] = masks.astype(jnp.int32)
    side = GROUP * PAIRS
    step = GROUP * EMB
    row, col = iota((side, PAIRS), 0), iota((side, PAIRS), 1)
    select = ones_where((row % EMB) * EMB + row // step == col)
    part = dot_nt(select, gate_ref[...]).astype(BF16)
    full = dot_nt(part, select)
    same = (iota((side, side), 0) // EMB) % GROUP == (iota((side, side), 1) // EMB) % GROUP
    gate_out[...] = jnp.where(same, full, 0.0).astype(BF16)
    row, col = iota((PAIRS, PAIRS), 0), iota((PAIRS, PAIRS), 1)
    order = (row % EMB) * EMB + row // EMB == col
    column = jnp.sum(jnp.where(order, bias_ref[...], 0.0), axis=1, keepdims=True)
    bias_out[...] = jnp.broadcast_to(column, bias_out.shape)


def plan(owner, item, request, probes, gate_weight, gate_bias, size):
    rows = owner.shape[1]
    return pl.pallas_call(
        plan_kernel,
        out_shape=(
            jax.ShapeDtypeStruct((size, 3 * LANES), jnp.int32),
            jax.ShapeDtypeStruct((1, rows), jnp.int32),
            jax.ShapeDtypeStruct((GROUP * PAIRS, GROUP * PAIRS), BF16),
            jax.ShapeDtypeStruct((PAIRS, LANES), F32),
        ),
        compiler_params=pltpu.CompilerParams(vmem_limit_bytes=VMEM),
        name="plan",
    )(owner, item, request, probes, gate_weight, gate_bias)


def score_kernel(query_ref, items_ref, gate_ref, bias_ref, scores_ref,
                 dots_a, dots_b, logits_a, logits_b, num_ref, den_ref):
    query_rows = query_ref.shape[0]
    tiles = items_ref.shape[0] // TILE_COLS
    step = GROUP * EMB
    groups = query_rows // step
    row_blocks = query_rows // TILE_COLS

    def piece(tile, index, out):
        j, block = index // row_blocks, index % row_blocks
        start = pl.multiple_of(block * TILE_COLS, TILE_COLS)
        lanes = pl.multiple_of(j * D, D)
        values = dot_nt(
            query_ref[pl.ds(start, TILE_COLS), :],
            items_ref[tile * TILE_COLS : (tile + 1) * TILE_COLS, pl.ds(lanes, D)],
        )
        out[j, pl.ds(start, TILE_COLS), :] = (values * SCALE).astype(BF16)

    def gate(dots, group, out):
        start = pl.multiple_of(group * step, step)
        part = dots[:, pl.ds(start, step), :].reshape(GROUP * PAIRS, TILE_COLS)
        out[...] = dot(gate_ref[...], part)

    def mix(dots, group, logits):
        start = pl.multiple_of(group * step, step)
        num = jnp.zeros((step, TILE_COLS), F32)
        den = jnp.zeros((step, TILE_COLS), F32)
        for j in range(EMB):
            bias = bias_ref[j * EMB : (j + 1) * EMB, :]
            bias = jnp.concatenate([jnp.concatenate([bias] * GROUP, axis=0)] * 2, axis=1)
            logit = logits[j * step : (j + 1) * step, :] + bias
            power = jnp.exp2(jnp.minimum(logit * LOG2E, 126.0))
            weight = jnp.maximum(jnp.log(1.0 + power), logit)
            den = den + weight
            num = num + weight * dots[j, pl.ds(start, step), :].astype(F32)
        for half in range(TILE_COLS // LANES):
            lanes = slice(half * LANES, (half + 1) * LANES)
            num_ref[half, pl.ds(start, step), :] = num[:, lanes]
            den_ref[half, pl.ds(start, step), :] = den[:, lanes]

    buffers = (dots_a, dots_b)

    @pl.loop(0, groups)
    def _(index):
        piece(0, index, dots_a)

    for tile in range(tiles):
        dots, ahead = buffers[tile % 2], buffers[(tile + 1) % 2]
        gate(dots, 0, logits_a)

        @pl.loop(0, groups // 2)
        def _(pair):
            first = pair * 2
            if tile + 1 < tiles:
                piece(tile + 1, first, ahead)
                piece(tile + 1, first + 1, ahead)
            gate(dots, first + 1, logits_b)
            mix(dots, first, logits_a)
            gate(dots, jnp.minimum(first + 2, groups - 1), logits_a)
            mix(dots, first + 1, logits_b)

        for half in range(TILE_COLS // LANES):
            num = jnp.zeros((query_rows // EMB, LANES), F32)
            den = jnp.ones((query_rows // EMB, LANES), F32)
            for i in range(EMB):
                num = num + num_ref[half, pl.ds(i, query_rows // EMB, stride=EMB), :]
                den = den + den_ref[half, pl.ds(i, query_rows // EMB, stride=EMB), :]
            start = tile * TILE_COLS + half * LANES
            scores_ref[start : start + LANES, :] = (num / den).T


def score(queries, items, gate_full, bias_full):
    query_rows, item_rows = queries.shape[0], items.shape[0]
    return pl.pallas_call(
        score_kernel,
        out_shape=jax.ShapeDtypeStruct((item_rows, query_rows // EMB), F32),
        scratch_shapes=[
            pltpu.VMEM((EMB, query_rows, TILE_COLS), BF16),
            pltpu.VMEM((EMB, query_rows, TILE_COLS), BF16),
            pltpu.VMEM((GROUP * PAIRS, TILE_COLS), F32),
            pltpu.VMEM((GROUP * PAIRS, TILE_COLS), F32),
            pltpu.VMEM((TILE_COLS // LANES, query_rows, LANES), F32),
            pltpu.VMEM((TILE_COLS // LANES, query_rows, LANES), F32),
        ],
        compiler_params=pltpu.CompilerParams(vmem_limit_bytes=VMEM),
        name="score",
    )(queries, items, gate_full, bias_full)


def batcher(count):
    pairs = []
    p = 1
    while p < count:
        k = p
        while k >= 1:
            for j in range(k % p, count - k, 2 * k):
                for i in range(min(k, count - j - k)):
                    if (i + j) // (2 * p) == (i + j + k) // (2 * p):
                        pairs.append((i + j, i + j + k))
            k //= 2
        p *= 2
    return pairs


def order_pair(values, i, j):
    values[i], values[j] = jnp.maximum(values[i], values[j]), jnp.minimum(values[i], values[j])


def clean(values):
    stride = len(values) // 2
    while stride:
        for i in range(len(values)):
            if not i & stride:
                order_pair(values, i, i + stride)
        stride //= 2


def clean_block(load, store, start, count):
    values = [load(start + i) for i in range(count)]
    clean(values)
    for i in range(count):
        store(start + i, values[i])


def sort_all(load, store, load_sorted, total, block):
    for start in range(0, total, block):
        values = [load(start + i) for i in range(block)]
        for i, j in batcher(block):
            order_pair(values, i, j)
        for i in range(block):
            store(start + i, values[i])
    size = 2 * block
    while size <= total:
        for start in range(0, total, size):
            if size == 2 * block:
                upper, lower = [], []
                for i in range(block):
                    a, b = load_sorted(start + i), load_sorted(start + size - 1 - i)
                    upper.append(jnp.maximum(a, b))
                    lower.append(jnp.minimum(a, b))
                for offset, values in ((0, upper), (block, lower[::-1])):
                    clean(values)
                    for i in range(block):
                        store(start + offset + i, values[i])
            else:
                half, quarter = size // 2, size // 4
                for i in range(quarter):
                    spots = (i, i + quarter, size - 1 - i - quarter, size - 1 - i)
                    values = [load_sorted(start + spot) for spot in spots]
                    order_pair(values, 0, 3)
                    order_pair(values, 1, 2)
                    order_pair(values, 0, 1)
                    order_pair(values, 2, 3)
                    for spot, value in zip(spots, values):
                        store(start + spot, value)
                for offset in range(0, size, quarter):
                    clean_block(load_sorted, store, start + offset, quarter)
        size *= 2


def merge_top(load, store, load_merged, partner, total):
    quarter = total // 4
    done = {}
    for i in range(quarter):
        spots = [i, i + quarter, i + 2 * quarter, i + 3 * quarter]
        values = [jnp.maximum(load(spot), partner(load(total - 1 - spot))) for spot in spots]
        order_pair(values, 0, 2)
        order_pair(values, 1, 3)
        order_pair(values, 0, 1)
        order_pair(values, 2, 3)
        for spot, value in zip(spots, values):
            store(spot, value)
    for offset in range(0, total, quarter):
        clean_block(load_merged, store, offset, quarter)


def rank_kernel(scores_ref, query_ref, items_ref, codes_ref, weight_hbm, bias_ref, out_weight_ref,
                result_ref, weight_ref, query_f32, user_ref, sort_a, sort_b, best_ref, weight_sem,
                *, fetch):
    copy = pltpu.make_async_copy(weight_hbm, weight_ref, weight_sem)
    copy.start()
    size = codes_ref.shape[0]
    item_rows, requests = scores_ref.shape
    local = requests // size
    best_of(scores_ref, codes_ref, result_ref, sort_a, sort_b, best_ref, local)

    query_f32[...] = query_ref[...].astype(F32)
    for i in range(EMB):
        user_ref[:, i * D : (i + 1) * D] = query_f32[pl.ds(i, requests, stride=EMB), :].astype(BF16)
    scores_high, scores_low = split_two(scores_ref[...])
    copy.wait()
    total = size * fetch
    block = total // 3
    code_item = codes_ref[:, :LANES]
    digits = jnp.concatenate(
        [code_item // BASE, code_item % BASE, codes_ref[:, LANES : 2 * LANES]], axis=1
    ).astype(F32).astype(BF16)
    answer = jnp.zeros((size, LANES), F32)
    for start in range(0, total, block):
        def source_of(shape, dim):
            row = (iota(shape, dim) + start).astype(F32)
            return jnp.floor((row + 0.5) * (1.0 / fetch))

        from_source = ones_where(source_of((block, size), 0) == iota((block, size), 1).astype(F32))
        taken = dot(from_source, digits)
        slot = iota((block, LANES), 0) + start - source_of((block, LANES), 0).astype(jnp.int32) * fetch
        mine = slot == iota((block, LANES), 1)
        item = jnp.sum(
            jnp.where(mine, taken[:, :LANES] * BASE + taken[:, LANES : 2 * LANES], 0.0),
            axis=1, keepdims=True,
        ).astype(jnp.int32)
        request = jnp.sum(
            jnp.where(mine, taken[:, 2 * LANES :], 0.0), axis=1, keepdims=True
        ).astype(jnp.int32)
        pick_item = ones_where(item == iota((block, item_rows), 1))
        asked = request == iota((block, requests), 1)
        pick_user = ones_where(asked)
        first = dot(pick_item, items_ref[...]) + dot(pick_user, user_ref[...])
        state = first
        for layer in range(weight_ref.shape[0]):
            hidden = dot(state.astype(BF16), weight_ref[layer]) + bias_ref[layer : layer + 1, :]
            state = first * hidden + state
        mixed = dot(pick_item, scores_high) + dot(pick_item, scores_low)
        mixed = jnp.where(asked, mixed, 0.0)
        weighted = state * out_weight_ref[...]
        partial = sum(
            [weighted[:, i * LANES : (i + 1) * LANES] for i in range(1, weighted.shape[1] // LANES)],
            weighted[:, :LANES],
        )
        for i in range(requests // LANES):
            partial = partial + mixed[:, i * LANES : (i + 1) * LANES]
        column = jnp.sum(partial, axis=1, keepdims=True)
        placed = jnp.where(mine, column, 0.0)
        to_source = ones_where(source_of((size, block), 1) == iota((size, block), 0).astype(F32))
        high, rest = split_two(placed)
        middle, low = split_two(placed - high.astype(F32))
        answer = answer + (dot(to_source, high) + (dot(to_source, middle) + dot(to_source, low)))
    result_ref[:, local * LANES :] = answer


def best_of(scores_ref, codes_ref, result_ref, sort_a, sort_b, best_ref, local):
    size = codes_ref.shape[0]
    item_rows, requests = scores_ref.shape
    lists = item_rows // EMB
    masks = codes_ref[:, 2 * LANES :].astype(F32).astype(BF16)
    lane, from_row = iota((LANES, requests), 1), iota((LANES, requests), 0)
    source = iota((size, requests), 1) // local == iota((size, requests), 0)
    allowed = []
    for cluster in range(CL_DEV):
        spread = dot(masks, ones_where(from_row == cluster * local + lane % local))
        allowed.append(jnp.sum(jnp.where(source, spread, 0.0), axis=0, keepdims=True) > 0.5)
    for chunk in range(requests // LANES):
        lanes = slice(chunk * LANES, (chunk + 1) * LANES)
        fits = [jnp.broadcast_to(a[:, lanes], (EMB, LANES)) for a in allowed]

        def load(i):
            values = scores_ref[i * EMB : (i + 1) * EMB, lanes]
            return jnp.where(fits[i * CL_DEV // lists], values, -jnp.inf)

        def reader(ref):
            return lambda i: ref[i]

        def writer(ref):
            def store(i, value):
                ref[i] = value
            return store

        sort_all(load, writer(sort_a), reader(sort_a), lists, 32)
        held, other = sort_a, sort_b
        shift = EMB // 2
        while shift:
            merge_top(
                reader(held), writer(other), reader(other),
                functools.partial(pltpu.roll, shift=shift, axis=0), lists,
            )
            held, other = other, held
            shift //= 2
        for i in range(lists):
            best_ref[i : i + 1, :] = held[i][:1, :]
        best_ref[...] = best_ref[...].T
        per_chunk = LANES // local
        for r in range(local):
            result_ref[chunk * per_chunk : (chunk + 1) * per_chunk, r * LANES : (r + 1) * LANES] = (
                best_ref[pl.ds(r, per_chunk, stride=local), :]
            )


def rank(scores, queries, items, codes, cross_weight, cross_bias, out_weight, local, fetch):
    size = codes.shape[0]
    requests = scores.shape[1]
    vmem = pl.BlockSpec(memory_space=pltpu.VMEM)
    return pl.pallas_call(
        functools.partial(rank_kernel, fetch=fetch),
        out_shape=jax.ShapeDtypeStruct((size, (local + 1) * LANES), F32),
        in_specs=[vmem, vmem, vmem, vmem, pl.BlockSpec(memory_space=pl.ANY), vmem, vmem],
        out_specs=vmem,
        scratch_shapes=[
            pltpu.VMEM(cross_weight.shape, BF16),
            pltpu.VMEM(queries.shape, F32),
            pltpu.VMEM((requests, EMB * D), BF16),
            pltpu.VMEM((items.shape[0] // EMB, EMB, LANES), F32),
            pltpu.VMEM((items.shape[0] // EMB, EMB, LANES), F32),
            pltpu.VMEM((LANES, LANES), F32),
            pltpu.SemaphoreType.DMA,
        ],
        compiler_params=pltpu.CompilerParams(vmem_limit_bytes=VMEM),
        name="rank",
    )(scores, queries, items, codes, cross_weight, cross_bias, out_weight)


def merge_kernel(back_ref, owner_ref, place_ref, top_ref, rerank_ref, list_ref, merge_a, merge_b):
    size = back_ref.shape[0]
    local = back_ref.shape[1] // LANES - 1
    rows = owner_ref.shape[1]
    at = owner_ref[...] == iota((size, rows), 0)
    slots = ones_where(place_ref[...] == iota((LANES, rows), 0))
    answer = back_ref[:, local * LANES :]
    high, rest = split_two(answer)
    middle, low = split_two(answer - high.astype(F32))
    spread = dot(high, slots) + (dot(middle, slots) + dot(low, slots))
    rerank_ref[...] = jnp.sum(jnp.where(at, spread, 0.0), axis=0, keepdims=True)

    for r in range(local):
        list_ref[pl.ds(r, size, stride=local), :] = back_ref[:, r * LANES : (r + 1) * LANES]
    chunks = size * local // LANES
    merge_a[...] = list_ref[...].T

    def reader(ref, chunk=0):
        return lambda i: ref[i : i + 1, chunk * LANES : (chunk + 1) * LANES]

    def writer(ref):
        def store(i, value):
            ref[i : i + 1, :LANES] = value
        return store

    held, other = merge_a, merge_b
    while chunks > 1:
        half = chunks // 2
        for chunk in range(half):
            take = slice(chunk * LANES, (chunk + 1) * LANES)

            def load(i, ref=held, first=chunk, second=chunk + half):
                return ref[i : i + 1, first * LANES : (first + 1) * LANES]

            def store(i, value, ref=other, take=take):
                ref[i : i + 1, take] = value

            def read(i, ref=other, take=take):
                return ref[i : i + 1, take]

            merge_pairs(
                load,
                lambda i, ref=held, c=chunk + half: ref[i : i + 1, c * LANES : (c + 1) * LANES],
                store, read, LANES,
            )
        held, other = other, held
        chunks = half
    shift = LANES // 2
    while shift >= local:
        merge_top(
            reader(held), writer(other), reader(other),
            functools.partial(pltpu.roll, shift=LANES - shift, axis=1), LANES,
        )
        held, other = other, held
        shift //= 2
    top_ref[...] = held[:, :LANES].T[:local, :KEEP]


def merge_pairs(load, load_other, store, load_merged, total):
    for i in range(total):
        store(i, jnp.maximum(load(i), load_other(total - 1 - i)))
    quarter = total // 4
    for i in range(quarter):
        spots = [i, i + quarter, i + 2 * quarter, i + 3 * quarter]
        values = [load_merged(spot) for spot in spots]
        order_pair(values, 0, 2)
        order_pair(values, 1, 3)
        order_pair(values, 0, 1)
        order_pair(values, 2, 3)
        for spot, value in zip(spots, values):
            store(spot, value)
    for offset in range(0, total, quarter):
        clean_block(load_merged, store, offset, quarter)


def merge(back, owner, place):
    size = back.shape[0]
    local = back.shape[1] // LANES - 1
    return pl.pallas_call(
        merge_kernel,
        out_shape=(
            jax.ShapeDtypeStruct((local, KEEP), F32),
            jax.ShapeDtypeStruct(owner.shape, F32),
        ),
        scratch_shapes=[
            pltpu.VMEM((size * local, LANES), F32),
            pltpu.VMEM((LANES, size * local), F32),
            pltpu.VMEM((LANES, size * local), F32),
        ],
        compiler_params=pltpu.CompilerParams(vmem_limit_bytes=VMEM),
        name="merge",
    )(back, owner, place)


def exchange(x):
    return lax.all_to_all(x, "cand", split_axis=0, concat_axis=0, tiled=True)


def on_device(users, items, probes, gate_weight, gate_bias, cross_weight, cross_bias, out_weight,
              row_device, row_item, row_request):
    size = lax.axis_size("cand")
    local = users.shape[0]
    rows = row_item.shape[0]
    fetch = max(2, 2 * rows // size)
    own = users.reshape(1, local * EMB, D)
    queries = exchange(jnp.broadcast_to(own, (size, local * EMB, D)))
    queries = queries.reshape(size * local * EMB, D)
    owner = row_device.reshape(1, rows)
    codes, place, gate_full, bias_full = plan(
        owner, row_item.reshape(1, rows), row_request.reshape(1, rows), probes,
        gate_weight, gate_bias.reshape(1, PAIRS), size,
    )
    codes = exchange(codes)
    scores = score(queries, items, gate_full, bias_full)
    result = rank(
        scores, queries, items, codes, cross_weight, cross_bias, out_weight.reshape(1, -1),
        local, fetch,
    )
    top, rerank = merge(exchange(result), owner, place)
    return top, rerank.reshape(rows)


def solution(mesh):
    split_rows = P(("groups", "cand"), None)
    split = P(("groups", "cand"))
    return jax.shard_map(
        on_device,
        mesh=mesh,
        in_specs=(split_rows, split_rows, split_rows, P(), P(), P(), P(), P(), split_rows, split, split),
        out_specs=(split_rows, split),
        check_vma=False,
    )
```

profile of v0, /device:TPU:0, one launch (start us, length us, event | category | flops | bytes accessed | tf_op | source)
XLA Modules:
  0.0 117.1 jit_solution(8152770261293025170)
XLA Ops:
  0.6 1.3 %reshape.33.item_ref = s32[1,768]{1,0:T(1,128)} reshape(s32[768]{0:T(1024)} %param.20) | data formatting | bytes 6144 | tf_op jit(solution)/shard_map/reshape | solution.py:529
  1.9 1.3 %reshape.34.request_ref = s32[1,768]{1,0:T(1,128)} reshape(s32[768]{0:T(1024)} %param.21) | data formatting | bytes 6144 | tf_op jit(solution)/shard_map/reshape | solution.py:529
  3.2 1.9 %plan.1 = (s32[32,384]{1,0:T(8,128)}, s32[1,768]{1,0:T(1,128)}, bf16[256,256]{1,0:T(8,128)(2,1)}, f32[64,128]{1,0:T(8,128)}) custom-call(s32[1,768]{1,0:T(1,128)} %bitcast.18, s32[1,768]{1,0:T(1,128)} %reshape.33.item_ref, s32[1,768]{1,0:T(1,128)} %reshape.34.request_ref, s32[4,32]{1,0:T(4,128)} %probes_ref.1, bf16[64,64]{1,0:T(8,128)(2,1)} %gate_ref.1, ...), custom_call_target="tpu_custom_call" | custom-call | tf_op jit(solution)/shard_map/plan/pallas_call | solution.py:97
  5.1 1.5 %copy.13 = s32[32,1,384]{2,1,0:T(1,128)} copy(s32[32,1,384]{2,0,1:T(8,128)} %bitcast.17) | data formatting | bytes 98304 | tf_op jit(solution)/shard_map/all_to_all | solution.py:515
  6.5 7.3 %all-to-all-start.1 = ((s32[32,1,384]{2,1,0:T(1,128)}), s32[32,1,384]{2,1,0:T(1,128)S(1)}, u32[]{:S(2)}, u32[]{:S(2)}) async-start(s32[32,1,384]{2,1,0:T(1,128)} %copy.13), calls=%async_computation.1 | async-start | bytes 98304 | tf_op jit(solution)/shard_map/all_to_all | solution.py:515
  13.8 0.7 broadcast_in_dim.7
  14.6 6.6 %all-to-all-done.1 = s32[32,1,384]{2,1,0:T(1,128)S(1)} async-done(((s32[32,1,384]{2,1,0:T(1,128)}), s32[32,1,384]{2,1,0:T(1,128)S(1)}, u32[]{:S(2)}, u32[]{:S(2)}) %all-to-all-start.1) | async-done | bytes 49184 | tf_op jit(solution)/shard_map/all_to_all | solution.py:515
  21.2 0.7 broadcast_in_dim.8
  21.9 2.6 %all-to-all-start = ((bf16[32,32,128]{2,1,0:T(8,128)(2,1)}), bf16[32,32,128]{2,1,0:T(8,128)(2,1)S(1)}, u32[]{:S(2)}, u32[]{:S(2)}) async-start(bf16[32,32,128]{2,1,0:T(8,128)(2,1)} %broadcast_in_dim.8), calls=%async_computation | async-start | bytes 524288 | tf_op jit(solution)/shard_map/all_to_all | solution.py:515
  24.5 0.6 copy.20
  25.1 10.0 %all-to-all-done = bf16[32,32,128]{2,1,0:T(8,128)(2,1)S(1)} async-done(((bf16[32,32,128]{2,1,0:T(8,128)(2,1)}), bf16[32,32,128]{2,1,0:T(8,128)(2,1)S(1)}, u32[]{:S(2)}, u32[]{:S(2)}) %all-to-all-start) | async-done | bytes 262176 | tf_op jit(solution)/shard_map/all_to_all | solution.py:515
  35.1 0.0 copy-start
  35.1 0.7 copy-done
  35.8 37.7 %score.1.scores_ref = f32[1024,128]{1,0:T(8,128)} custom-call(bf16[1024,128]{1,0:T(8,128)(2,1)} %bitcast.12, bf16[1024,1024]{1,0:T(8,128)(2,1)} %items_ref.3, bf16[256,256]{1,0:T(8,128)(2,1)} %get-tuple-element.8.gate_ref, f32[64,128]{1,0:T(8,128)} %get-tuple-element.9.bias_ref), custom_call_target="tpu_custom_call" | custom-call | tf_op jit(solution)/shard_map/score/pallas_call | solution.py:183
  73.5 27.8 %rank.1 = f32[32,640]{1,0:T(8,128)} custom-call(f32[1024,128]{1,0:T(8,128)} %score.1.scores_ref, bf16[1024,128]{1,0:T(8,128)(2,1)} %bitcast.13, bf16[1024,1024]{1,0:T(8,128)(2,1)} %items_ref.3, s32[32,384]{1,0:T(8,128)} %bitcast.16, bf16[3,1024,1024]{2,1,0:T(8,128)(2,1)} %weight_hbm.1, f32[3,1024]{1,0:T(4,128)} %bias_ref.1, f32[1,1024]{1,0:T(1,128)} %bitcast.20), custom_call_target="tpu_custom_call" | custom-call | tf_op jit(solution)/shard_map/rank/pallas_call | solution.py:401
  101.3 1.0 copy.14
  102.3 9.7 %all_to_all.27 = f32[32,1,640]{2,1,0:T(1,128)S(1)} all-to-all(f32[32,1,640]{2,1,0:T(1,128)S(1)} %copy.14), channel_id=1, replica_groups=mesh['groups'=1,'cand'=32] {'cand'}, dimensions={0} | all-to-all | bytes 163840 | tf_op jit(solution)/shard_map/all_to_all | solution.py:515
  112.0 0.6 copy.19
  112.6 3.2 %merge.1 = (f32[4,96]{1,0:T(4,128)}, f32[1,768]{1,0:T(1,128)}) custom-call(f32[32,640]{1,0:T(8,128)} %bitcast.15, s32[1,768]{1,0:T(1,128)} %bitcast.19, s32[1,768]{1,0:T(1,128)} %get-tuple-element.11.place_ref), custom_call_target="tpu_custom_call" | custom-call | tf_op jit(solution)/shard_map/merge/pallas_call | solution.py:498
  115.8 1.3 %reduce = f32[768]{0:T(1024)} reduce(f32[1,768]{1,0:T(1,128)} %get-tuple-element.13, f32[]{:T(128)} %constant.2), dimensions={0}, to_apply=%get-tuple-element.13.reduce_sub_computation | reduce | bytes 6148 | tf_op jit(solution)/shard_map/merge/pallas_call | solution.py:498
Async XLA Ops:
  6.5 14.6 %all-to-all-start.1 = ((s32[32,1,384]{2,1,0:T(1,128)}), s32[32,1,384]{2,1,0:T(1,128)S(1)}, u32[]{:S(2)}, u32[]{:S(2)}) async-start(s32[32,1,384]{2,1,0:T(1,128)} %copy.13), calls=%async_computation.1 | async-start | bytes 98304 | tf_op jit(solution)/shard_map/all_to_all | solution.py:515
  21.9 13.2 %all-to-all-start = ((bf16[32,32,128]{2,1,0:T(8,128)(2,1)}), bf16[32,32,128]{2,1,0:T(8,128)(2,1)S(1)}, u32[]{:S(2)}, u32[]{:S(2)}) async-start(bf16[32,32,128]{2,1,0:T(8,128)(2,1)} %broadcast_in_dim.8), calls=%async_computation | async-start | bytes 524288 | tf_op jit(solution)/shard_map/all_to_all | solution.py:515
  35.1 0.7 copy-start
where the time goes:
time: 118 us; the launch traced here: 117 us
  Pallas kernels  70.6 us (60%)
  waiting for transfers between devices  16.6 us (14%)
  starting transfers between devices  9.88 us (8%)
  blocking collectives  9.72 us (8%)
  local copies, waits for them, and re-layouts  8.37 us (7%)
  other arithmetic  1.26 us (1%)
    pallas_call x1, Pallas kernels, score(): pl.pallas_call(score_kernel, out_shape=jax.ShapeDtypeStruct((item_rows, q...  37.7 us
    pallas_call x1, Pallas kernels, rank(): pl.pallas_call(functools.partial(rank_kernel, fetch=fetch), out_shape=jax...  27.8 us
    all_to_all x2, waiting for transfers between devices, exchange(): return lax.all_to_all(x, 'cand', split_axis=0, concat_axis=0, tiled=True)  16.6 us
    all_to_all x2, starting transfers between devices, exchange(): return lax.all_to_all(x, 'cand', split_axis=0, concat_axis=0, tiled=True)  9.88 us
    all_to_all x1, blocking collectives, exchange(): return lax.all_to_all(x, 'cand', split_axis=0, concat_axis=0, tiled=True)  9.72 us
    pallas_call x1, Pallas kernels, merge(): pl.pallas_call(merge_kernel, out_shape=(jax.ShapeDtypeStruct((local, KEEP...  3.16 us
    all_to_all x2, local copies, waits for them, and re-layouts, exchange(): return lax.all_to_all(x, 'cand', split_axis=0, concat_axis=0, tiled=True)  2.43 us
  transfers between devices with their start and end apart: 2, of which 2 were waited for; matrix products, arithmetic and copies ran while one was open for 1% of the time, Pallas kernels for 0%

commit v1 on v0

--- a/solution.py
+++ b/solution.py
@@ -16,6 +16,10 @@
 CL_DEV = 2
 REQ_DEV = 4
 LANES = 128
+SUBLANES = 4
+BLOCKS = 2
+COLUMNS = 256
+NEVER = -1e30
 TILE_COLS = 256
 GROUP = 4
 BASE = 32
@@ -44,6 +48,17 @@
     return jnp.where(cond, 1.0, 0.0).astype(BF16)
 
 
+def message(row, size):
+    return pl.ds(row, size, stride=SUBLANES)
+
+
+def tree_sum(values):
+    values = [(a + b).astype(F32) for a, b in zip(values[::2], values[1::2])]
+    while len(values) > 1:
+        values = [a + b for a, b in zip(values[::2], values[1::2])]
+    return values[0]
+
+
 def split_two(x):
     high = x.astype(BF16)
     return high, (x - high.astype(F32)).astype(BF16)
@@ -52,7 +67,7 @@
 def plan_kernel(owner_ref, item_ref, request_ref, probes_ref, gate_ref, bias_ref,
                 codes_ref, place_ref, gate_out, bias_out):
     rows = owner_ref.shape[1]
-    size = codes_ref.shape[0]
+    size = codes_ref.shape[0] // SUBLANES
     at = owner_ref[...] == iota((size, rows), 0)
     at_one = ones_where(at)
     before = ones_where(iota((rows, rows), 0) < iota((rows, rows), 1))
@@ -66,8 +81,10 @@
         [jnp.where(at, value.astype(F32), 0.0).astype(BF16) for value in values], axis=0
     )
     codes = dot_nt(spread, slots)
-    codes_ref[:, :LANES] = (codes[:size] * BASE + codes[size : 2 * size]).astype(jnp.int32)
-    codes_ref[:, LANES : 2 * LANES] = codes[2 * size :].astype(jnp.int32)
+    codes_ref[...] = jnp.zeros_like(codes_ref)
+    items = (codes[:size] * BASE + codes[size : 2 * size]).astype(jnp.int32)
+    codes_ref[message(0, size), :] = items
+    codes_ref[message(1, size), :] = codes[2 * size :].astype(jnp.int32)
     requests, probes = probes_ref.shape
     lane = iota((size, LANES), 1)
     masks = jnp.zeros((size, LANES), F32)
@@ -77,7 +94,7 @@
             hit = jnp.where(probes_ref[request : request + 1, :] == ids, 1.0, 0.0)
             any_hit = jnp.max(hit, axis=1, keepdims=True)
             masks = jnp.where(lane == cluster * requests + request, any_hit, masks)
-    codes_ref[:, 2 * LANES :] = masks.astype(jnp.int32)
+    codes_ref[message(2, size), :] = masks.astype(jnp.int32)
     side = GROUP * PAIRS
     step = GROUP * EMB
     row, col = iota((side, PAIRS), 0), iota((side, PAIRS), 1)
@@ -86,10 +103,9 @@
     full = dot_nt(part, select)
     same = (iota((side, side), 0) // EMB) % GROUP == (iota((side, side), 1) // EMB) % GROUP
     gate_out[...] = jnp.where(same, full, 0.0).astype(BF16)
-    row, col = iota((PAIRS, PAIRS), 0), iota((PAIRS, PAIRS), 1)
-    order = (row % EMB) * EMB + row // EMB == col
+    order = (row % EMB) * EMB + row // step == col
     column = jnp.sum(jnp.where(order, bias_ref[...], 0.0), axis=1, keepdims=True)
-    bias_out[...] = jnp.broadcast_to(column, bias_out.shape)
+    bias_out[...] = jnp.broadcast_to(column, bias_out.shape).astype(BF16)
 
 
 def plan(owner, item, request, probes, gate_weight, gate_bias, size):
@@ -97,10 +113,10 @@
     return pl.pallas_call(
         plan_kernel,
         out_shape=(
-            jax.ShapeDtypeStruct((size, 3 * LANES), jnp.int32),
+            jax.ShapeDtypeStruct((size * SUBLANES, LANES), jnp.int32),
             jax.ShapeDtypeStruct((1, rows), jnp.int32),
             jax.ShapeDtypeStruct((GROUP * PAIRS, GROUP * PAIRS), BF16),
-            jax.ShapeDtypeStruct((PAIRS, LANES), F32),
+            jax.ShapeDtypeStruct((GROUP * PAIRS, LANES), BF16),
         ),
         compiler_params=pltpu.CompilerParams(vmem_limit_bytes=VMEM),
         name="plan",
@@ -108,7 +124,7 @@
 
 
 def score_kernel(query_ref, items_ref, gate_ref, bias_ref, scores_ref,
-                 dots_a, dots_b, logits_a, logits_b, num_ref, den_ref):
+                 dots_a, dots_b, num_ref, den_ref, *logits):
     query_rows = query_ref.shape[0]
     tiles = items_ref.shape[0] // TILE_COLS
     step = GROUP * EMB
@@ -128,20 +144,20 @@
     def gate(dots, group, out):
         start = pl.multiple_of(group * step, step)
         part = dots[:, pl.ds(start, step), :].reshape(GROUP * PAIRS, TILE_COLS)
-        out[...] = dot(gate_ref[...], part)
+        out[...] = dot(gate_ref[...], part).astype(BF16)
 
     def mix(dots, group, logits):
         start = pl.multiple_of(group * step, step)
-        num = jnp.zeros((step, TILE_COLS), F32)
-        den = jnp.zeros((step, TILE_COLS), F32)
+        weights, products = [], []
         for j in range(EMB):
-            bias = bias_ref[j * EMB : (j + 1) * EMB, :]
-            bias = jnp.concatenate([jnp.concatenate([bias] * GROUP, axis=0)] * 2, axis=1)
-            logit = logits[j * step : (j + 1) * step, :] + bias
+            bias = bias_ref[j * step : (j + 1) * step, :]
+            logit = logits[j * step : (j + 1) * step, :] + jnp.concatenate([bias, bias], axis=1)
             power = jnp.exp2(jnp.minimum(logit * LOG2E, 126.0))
             weight = jnp.maximum(jnp.log(1.0 + power), logit)
-            den = den + weight
-            num = num + weight * dots[j, pl.ds(start, step), :].astype(F32)
+            weights.append(weight)
+            products.append(weight * dots[j, pl.ds(start, step), :])
+        den = tree_sum(weights)
+        num = tree_sum(products)
         for half in range(TILE_COLS // LANES):
             lanes = slice(half * LANES, (half + 1) * LANES)
             num_ref[half, pl.ds(start, step), :] = num[:, lanes]
@@ -155,18 +171,21 @@
 
     for tile in range(tiles):
         dots, ahead = buffers[tile % 2], buffers[(tile + 1) % 2]
-        gate(dots, 0, logits_a)
-
-        @pl.loop(0, groups // 2)
-        def _(pair):
-            first = pair * 2
-            if tile + 1 < tiles:
-                piece(tile + 1, first, ahead)
-                piece(tile + 1, first + 1, ahead)
-            gate(dots, first + 1, logits_b)
-            mix(dots, first, logits_a)
-            gate(dots, jnp.minimum(first + 2, groups - 1), logits_a)
-            mix(dots, first + 1, logits_b)
+        gate(dots, 0, logits[0])
+        gate(dots, 1, logits[1])
+
+        @pl.loop(0, groups // 8)
+        def _(quad):
+            for phase in range(4):
+                first = quad * 8 + phase * 2
+                here, there = logits[2 * (phase % 2) : 2 * (phase % 2) + 2], logits[2 - 2 * (phase % 2) : 4 - 2 * (phase % 2)]
+                if tile + 1 < tiles:
+                    piece(tile + 1, first, ahead)
+                    piece(tile + 1, first + 1, ahead)
+                for k in range(2):
+                    gate(dots, jnp.minimum(first + 2 + k, groups - 1), there[k])
+                for k in range(2):
+                    mix(dots, first + k, here[k])
 
         for half in range(TILE_COLS // LANES):
             num = jnp.zeros((query_rows // EMB, LANES), F32)
@@ -186,11 +205,10 @@
         scratch_shapes=[
             pltpu.VMEM((EMB, query_rows, TILE_COLS), BF16),
             pltpu.VMEM((EMB, query_rows, TILE_COLS), BF16),
-            pltpu.VMEM((GROUP * PAIRS, TILE_COLS), F32),
-            pltpu.VMEM((GROUP * PAIRS, TILE_COLS), F32),
             pltpu.VMEM((TILE_COLS // LANES, query_rows, LANES), F32),
             pltpu.VMEM((TILE_COLS // LANES, query_rows, LANES), F32),
-        ],
+        ]
+        + [pltpu.VMEM((GROUP * PAIRS, TILE_COLS), BF16) for _ in range(4)],
         compiler_params=pltpu.CompilerParams(vmem_limit_bytes=VMEM),
         name="score",
     )(queries, items, gate_full, bias_full)
@@ -283,29 +301,39 @@
         clean_block(load_merged, store, offset, quarter)
 
 
-def rank_kernel(scores_ref, query_ref, items_ref, codes_ref, weight_hbm, bias_ref, out_weight_ref,
-                result_ref, weight_ref, query_f32, user_ref, sort_a, sort_b, best_ref, weight_sem,
-                *, fetch):
-    copy = pltpu.make_async_copy(weight_hbm, weight_ref, weight_sem)
-    copy.start()
-    size = codes_ref.shape[0]
+def rank_kernel(scores_ref, query_ref, codes_ref, items_hbm, weight_hbm, bias_ref, out_weight_ref,
+                result_ref, weight_ref, table_ref, query_f32, pair_ref, sort_a, sort_b, best_ref,
+                pick_ref, first_ref, state_ref, round_a, round_b, weight_sem, items_sem, *, fetch):
     item_rows, requests = scores_ref.shape
+    weight_copy = pltpu.make_async_copy(weight_hbm, weight_ref, weight_sem)
+    items_copy = pltpu.make_async_copy(items_hbm, table_ref.at[pl.ds(0, item_rows), :], items_sem)
+    items_copy.start()
+    weight_copy.start()
+    size = codes_ref.shape[0] // SUBLANES
     local = requests // size
-    best_of(scores_ref, codes_ref, result_ref, sort_a, sort_b, best_ref, local)
 
     query_f32[...] = query_ref[...].astype(F32)
     for i in range(EMB):
-        user_ref[:, i * D : (i + 1) * D] = query_f32[pl.ds(i, requests, stride=EMB), :].astype(BF16)
-    scores_high, scores_low = split_two(scores_ref[...])
-    copy.wait()
+        users = query_f32[pl.ds(i, requests, stride=EMB), :].astype(BF16)
+        table_ref[item_rows:, i * D : (i + 1) * D] = users
+    pair_ref[:, :requests], pair_ref[:, requests:] = split_two(scores_ref[...])
+    items_copy.wait()
+    weight_copy.wait()
+    best_of(scores_ref, codes_ref, result_ref, sort_a, sort_b, best_ref, local)
+
     total = size * fetch
-    block = total // 3
-    code_item = codes_ref[:, :LANES]
+    block = total // BLOCKS
+    width = first_ref.shape[-1]
+    code_item = codes_ref[message(0, size), :]
     digits = jnp.concatenate(
-        [code_item // BASE, code_item % BASE, codes_ref[:, LANES : 2 * LANES]], axis=1
+        [code_item // BASE, code_item % BASE, codes_ref[message(1, size), :]], axis=1
     ).astype(F32).astype(BF16)
     answer = jnp.zeros((size, LANES), F32)
-    for start in range(0, total, block):
+    for part in range(BLOCKS):
+        start = part * block
+        pick, first, state = pick_ref.at[part], first_ref.at[part], state_ref.at[part]
+        rounded = (round_a.at[part], round_b.at[part])
+
         def source_of(shape, dim):
             row = (iota(shape, dim) + start).astype(F32)
             return jnp.floor((row + 0.5) * (1.0 / fetch))
@@ -321,37 +349,53 @@
         request = jnp.sum(
             jnp.where(mine, taken[:, 2 * LANES :], 0.0), axis=1, keepdims=True
         ).astype(jnp.int32)
-        pick_item = ones_where(item == iota((block, item_rows), 1))
         asked = request == iota((block, requests), 1)
-        pick_user = ones_where(asked)
-        first = dot(pick_item, items_ref[...]) + dot(pick_user, user_ref[...])
-        state = first
-        for layer in range(weight_ref.shape[0]):
-            hidden = dot(state.astype(BF16), weight_ref[layer]) + bias_ref[layer : layer + 1, :]
-            state = first * hidden + state
-        mixed = dot(pick_item, scores_high) + dot(pick_item, scores_low)
-        mixed = jnp.where(asked, mixed, 0.0)
-        weighted = state * out_weight_ref[...]
-        partial = sum(
-            [weighted[:, i * LANES : (i + 1) * LANES] for i in range(1, weighted.shape[1] // LANES)],
-            weighted[:, :LANES],
-        )
-        for i in range(requests // LANES):
+        pick[:, :item_rows] = ones_where(item == iota((block, item_rows), 1))
+        pick[:, item_rows:] = ones_where(asked)
+        mixed = dot(pick[:, :item_rows], pair_ref[...])
+        mixed = jnp.where(asked, mixed[:, :requests] + mixed[:, requests:], 0.0)
+        partial = mixed[:, :LANES]
+        for i in range(1, requests // LANES):
             partial = partial + mixed[:, i * LANES : (i + 1) * LANES]
+
+        for column in range(0, width, COLUMNS):
+            columns = slice(column, column + COLUMNS)
+            values = dot(pick[...], table_ref[:, columns])
+            first[:, columns] = values
+            rounded[0][:, columns] = values.astype(BF16)
+        layers = weight_ref.shape[0]
+        for layer in range(layers):
+            for column in range(0, width, COLUMNS):
+                columns = slice(column, column + COLUMNS)
+                hidden = dot(rounded[layer % 2][...], weight_ref[layer, :, columns])
+                hidden = hidden + bias_ref[layer : layer + 1, columns]
+                before = (state if layer else first)[:, columns]
+                after = first[:, columns] * hidden + before
+                if layer + 1 < layers:
+                    state[:, columns] = after
+                    rounded[(layer + 1) % 2][:, columns] = after.astype(BF16)
+                else:
+                    weighted = after * out_weight_ref[:, columns]
+                    for i in range(COLUMNS // LANES):
+                        partial = partial + weighted[:, i * LANES : (i + 1) * LANES]
         column = jnp.sum(partial, axis=1, keepdims=True)
         placed = jnp.where(mine, column, 0.0)
         to_source = ones_where(source_of((size, block), 1) == iota((size, block), 0).astype(F32))
         high, rest = split_two(placed)
         middle, low = split_two(placed - high.astype(F32))
         answer = answer + (dot(to_source, high) + (dot(to_source, middle) + dot(to_source, low)))
-    result_ref[:, local * LANES :] = answer
+    spare = LANES - KEEP
+    free = iota(answer.shape, 1) >= KEEP
+    for row in range(local):
+        moved = pltpu.roll(answer, (KEEP - row * spare) % LANES, 1)
+        result_ref[message(row, size), :] = jnp.where(free, moved, result_ref[message(row, size), :])
 
 
 def best_of(scores_ref, codes_ref, result_ref, sort_a, sort_b, best_ref, local):
-    size = codes_ref.shape[0]
+    size = codes_ref.shape[0] // SUBLANES
     item_rows, requests = scores_ref.shape
     lists = item_rows // EMB
-    masks = codes_ref[:, 2 * LANES :].astype(F32).astype(BF16)
+    masks = codes_ref[message(2, size), :].astype(F32).astype(BF16)
     lane, from_row = iota((LANES, requests), 1), iota((LANES, requests), 0)
     source = iota((size, requests), 1) // local == iota((size, requests), 0)
     allowed = []
@@ -364,7 +408,7 @@
 
         def load(i):
             values = scores_ref[i * EMB : (i + 1) * EMB, lanes]
-            return jnp.where(fits[i * CL_DEV // lists], values, -jnp.inf)
+            return jnp.where(fits[i * CL_DEV // lists], values, NEVER)
 
         def reader(ref):
             return lambda i: ref[i]
@@ -389,48 +433,65 @@
         best_ref[...] = best_ref[...].T
         per_chunk = LANES // local
         for r in range(local):
-            result_ref[chunk * per_chunk : (chunk + 1) * per_chunk, r * LANES : (r + 1) * LANES] = (
+            start = chunk * per_chunk * SUBLANES + r
+            result_ref[pl.ds(start, per_chunk, stride=SUBLANES), :] = (
                 best_ref[pl.ds(r, per_chunk, stride=local), :]
             )
 
 
-def rank(scores, queries, items, codes, cross_weight, cross_bias, out_weight, local, fetch):
-    size = codes.shape[0]
+def rank(scores, queries, items, codes, cross_weight, cross_bias, out_weight, fetch):
     requests = scores.shape[1]
     vmem = pl.BlockSpec(memory_space=pltpu.VMEM)
+    item_rows, width = items.shape
+    total = codes.shape[0] // SUBLANES * fetch
+    block = (BLOCKS, total // BLOCKS)
+    anywhere = pl.BlockSpec(memory_space=pl.ANY)
     return pl.pallas_call(
         functools.partial(rank_kernel, fetch=fetch),
-        out_shape=jax.ShapeDtypeStruct((size, (local + 1) * LANES), F32),
-        in_specs=[vmem, vmem, vmem, vmem, pl.BlockSpec(memory_space=pl.ANY), vmem, vmem],
+        out_shape=jax.ShapeDtypeStruct(codes.shape, F32),
+        in_specs=[vmem, vmem, vmem, anywhere, anywhere, vmem, vmem],
         out_specs=vmem,
         scratch_shapes=[
             pltpu.VMEM(cross_weight.shape, BF16),
+            pltpu.VMEM((item_rows + requests, width), BF16),
             pltpu.VMEM(queries.shape, F32),
-            pltpu.VMEM((requests, EMB * D), BF16),
-            pltpu.VMEM((items.shape[0] // EMB, EMB, LANES), F32),
-            pltpu.VMEM((items.shape[0] // EMB, EMB, LANES), F32),
+            pltpu.VMEM((item_rows, 2 * requests), BF16),
+            pltpu.VMEM((item_rows // EMB, EMB, LANES), F32),
+            pltpu.VMEM((item_rows // EMB, EMB, LANES), F32),
             pltpu.VMEM((LANES, LANES), F32),
+            pltpu.VMEM((*block, item_rows + requests), BF16),
+            pltpu.VMEM((*block, width), F32),
+            pltpu.VMEM((*block, width), F32),
+            pltpu.VMEM((*block, width), BF16),
+            pltpu.VMEM((*block, width), BF16),
+            pltpu.SemaphoreType.DMA,
             pltpu.SemaphoreType.DMA,
         ],
         compiler_params=pltpu.CompilerParams(vmem_limit_bytes=VMEM),
         name="rank",
-    )(scores, queries, items, codes, cross_weight, cross_bias, out_weight)
+    )(scores, queries, codes, items, cross_weight, cross_bias, out_weight)
 
 
 def merge_kernel(back_ref, owner_ref, place_ref, top_ref, rerank_ref, list_ref, merge_a, merge_b):
-    size = back_ref.shape[0]
-    local = back_ref.shape[1] // LANES - 1
+    size = back_ref.shape[0] // SUBLANES
+    local = top_ref.shape[0]
     rows = owner_ref.shape[1]
     at = owner_ref[...] == iota((size, rows), 0)
-    slots = ones_where(place_ref[...] == iota((LANES, rows), 0))
-    answer = back_ref[:, local * LANES :]
-    high, rest = split_two(answer)
-    middle, low = split_two(answer - high.astype(F32))
-    spread = dot(high, slots) + (dot(middle, slots) + dot(low, slots))
-    rerank_ref[...] = jnp.sum(jnp.where(at, spread, 0.0), axis=0, keepdims=True)
+    spread = jnp.zeros((size, rows), F32)
+    spare = LANES - KEEP
+    for row in range(local):
+        lane = iota((LANES, rows), 0)
+        held = jnp.where(lane >= KEEP, lane - KEEP + row * spare, -1)
+        slots = ones_where(place_ref[...] == held)
+        answer = back_ref[message(row, size), :]
+        high, rest = split_two(answer)
+        middle, low = split_two(answer - high.astype(F32))
+        spread = spread + (dot(high, slots) + (dot(middle, slots) + dot(low, slots)))
+    rerank_ref[...] = jnp.sum(jnp.where(at, spread, 0.0), axis=0)
 
     for r in range(local):
-        list_ref[pl.ds(r, size, stride=local), :] = back_ref[:, r * LANES : (r + 1) * LANES]
+        best = back_ref[message(r, size), :]
+        list_ref[pl.ds(r, size, stride=local), :] = jnp.where(iota(best.shape, 1) < KEEP, best, NEVER)
     chunks = size * local // LANES
     merge_a[...] = list_ref[...].T
 
@@ -492,14 +553,13 @@
         clean_block(load_merged, store, offset, quarter)
 
 
-def merge(back, owner, place):
-    size = back.shape[0]
-    local = back.shape[1] // LANES - 1
+def merge(back, owner, place, local):
+    size = back.shape[0] // SUBLANES
     return pl.pallas_call(
         merge_kernel,
         out_shape=(
             jax.ShapeDtypeStruct((local, KEEP), F32),
-            jax.ShapeDtypeStruct(owner.shape, F32),
+            jax.ShapeDtypeStruct(owner.shape[1:], F32),
         ),
         scratch_shapes=[
             pltpu.VMEM((size * local, LANES), F32),
@@ -529,14 +589,13 @@
         owner, row_item.reshape(1, rows), row_request.reshape(1, rows), probes,
         gate_weight, gate_bias.reshape(1, PAIRS), size,
     )
+    queries, codes = lax.optimization_barrier((queries, codes))
     codes = exchange(codes)
     scores = score(queries, items, gate_full, bias_full)
     result = rank(
-        scores, queries, items, codes, cross_weight, cross_bias, out_weight.reshape(1, -1),
-        local, fetch,
+        scores, queries, items, codes, cross_weight, cross_bias, out_weight.reshape(1, -1), fetch
     )
-    top, rerank = merge(exchange(result), owner, place)
-    return top, rerank.reshape(rows)
+    return merge(exchange(result), owner, place, local)
 
 
 def solution(mesh):

time: 118 us -> 90.9 us (0.77)
  Pallas kernels: 70.6 us -> 55.7 us
  waiting for transfers between devices: 16.6 us -> 6.13 us
  local copies, waits for them, and re-layouts: 8.37 us -> 4.63 us
  blocking collectives: 9.72 us -> 13.4 us
  other arithmetic: 1.26 us -> 0 us
    all_to_all x2, waiting for transfers between devices: 16.6 us -> 6.13 us  [exchange(): return lax.all_to_all(x, 'cand', split_axis=0, concat_axis=0, tiled=True)]
    pallas_call x1, Pallas kernels: 37.7 us -> 27.5 us  [score(): pl.pallas_call(score_kernel, out_shape=jax.ShapeDtypeStruct((item_rows, q...]
    pallas_call x1, Pallas kernels: 27.8 us -> 23.2 us  [rank(): pl.pallas_call(functools.partial(rank_kernel, fetch=fetch), out_shape=jax...]
    all_to_all x1, blocking collectives: 9.72 us -> 13.4 us  [exchange(): return lax.all_to_all(x, 'cand', split_axis=0, concat_axis=0, tiled=True)]
    all_to_all x2 -> x0, local copies, waits for them, and re-layouts: 2.43 us -> none  [exchange(): return lax.all_to_all(x, 'cand', split_axis=0, concat_axis=0, tiled=True)]
    unnamed x4, local copies, waits for them, and re-layouts: 1.95 us -> 0.64 us
    pallas_call x1 -> x0, other arithmetic: 1.26 us -> none  [merge(): pl.pallas_call(merge_kernel, out_shape=(jax.ShapeDtypeStruct((local, KEEP...]
  transfers between devices with their start and end apart: 2 -> 2, of which waited for: 2 -> 1; matrix products, arithmetic and copies ran while one was open for 1% -> 3% of each run, Pallas kernels for 0% -> 33%
where the time goes in v1:
time: 90.9 us; the launch traced here: 90.4 us
  Pallas kernels  55.7 us (61%)
  blocking collectives  13.4 us (15%)
  starting transfers between devices  9.86 us (11%)
  waiting for transfers between devices  6.13 us (7%)
  local copies, waits for them, and re-layouts  4.63 us (5%)
    pallas_call x1, Pallas kernels, score(): pl.pallas_call(score_kernel, out_shape=jax.ShapeDtypeStruct((item_rows, q...  27.5 us
    pallas_call x1, Pallas kernels, rank(): pl.pallas_call(functools.partial(rank_kernel, fetch=fetch), out_shape=jax...  23.2 us
    all_to_all x1, blocking collectives, exchange(): return lax.all_to_all(x, 'cand', split_axis=0, concat_axis=0, tiled=True)  13.4 us
    all_to_all x2, starting transfers between devices, exchange(): return lax.all_to_all(x, 'cand', split_axis=0, concat_axis=0, tiled=True)  9.86 us
    all_to_all x2, waiting for transfers between devices, exchange(): return lax.all_to_all(x, 'cand', split_axis=0, concat_axis=0, tiled=True)  6.13 us
    pallas_call x1, Pallas kernels, merge(): pl.pallas_call(merge_kernel, out_shape=(jax.ShapeDtypeStruct((local, KEEP...  3.15 us
    pallas_call x1, Pallas kernels, plan(): pl.pallas_call(plan_kernel, out_shape=(jax.ShapeDtypeStruct((size * SUBLA...  1.92 us
  transfers between devices with their start and end apart: 2, of which 1 were waited for; matrix products, arithmetic and copies ran while one was open for 3% of the time, Pallas kernels for 33%

profile of v1, /device:TPU:0, one launch (start us, length us, event | category | flops | bytes accessed | tf_op | source)
XLA Modules:
  0.0 90.4 jit_solution(10657640388933754756)
XLA Ops:
  0.6 0.7 broadcast_in_dim.7
  1.3 0.7 broadcast_in_dim.8
  2.1 7.3 %all-to-all-start = ((bf16[32,32,128]{2,1,0:T(8,128)(2,1)}), bf16[32,32,128]{2,1,0:T(8,128)(2,1)S(1)}, u32[]{:S(2)}, u32[]{:S(2)}) async-start(bf16[32,32,128]{2,1,0:T(8,128)(2,1)} %broadcast_in_dim.8), calls=%async_computation | async-start | bytes 524288 | tf_op jit(solution)/shard_map/all_to_all | solution.py:575
  9.4 1.3 %reshape.30.item_ref = s32[1,768]{1,0:T(1,128)} reshape(s32[768]{0:T(1024)} %param.20) | data formatting | bytes 6144 | tf_op jit(solution)/shard_map/reshape | solution.py:589
  10.7 1.3 %reshape.31.request_ref = s32[1,768]{1,0:T(1,128)} reshape(s32[768]{0:T(1024)} %param.21) | data formatting | bytes 6144 | tf_op jit(solution)/shard_map/reshape | solution.py:589
  11.9 1.9 %plan.1 = (s32[128,128]{1,0:T(8,128)}, s32[1,768]{1,0:T(1,128)}, bf16[256,256]{1,0:T(8,128)(2,1)}, bf16[256,128]{1,0:T(8,128)(2,1)}) custom-call(s32[1,768]{1,0:T(1,128)} %bitcast.14, s32[1,768]{1,0:T(1,128)} %reshape.30.item_ref, s32[1,768]{1,0:T(1,128)} %reshape.31.request_ref, s32[4,32]{1,0:T(4,128)} %probes_ref.1, bf16[64,64]{1,0:T(8,128)(2,1)} %gate_ref.1, ...), custom_call_target="tpu_custom_call" | custom-call | tf_op jit(solution)/shard_map/plan/pallas_call | solution.py:113
  13.9 6.1 %all-to-all-done = bf16[32,32,128]{2,1,0:T(8,128)(2,1)S(1)} async-done(((bf16[32,32,128]{2,1,0:T(8,128)(2,1)}), bf16[32,32,128]{2,1,0:T(8,128)(2,1)S(1)}, u32[]{:S(2)}, u32[]{:S(2)}) %all-to-all-start) | async-done | bytes 262176 | tf_op jit(solution)/shard_map/all_to_all | solution.py:575
  20.0 0.0 copy-start
  20.0 2.6 %all-to-all-start.1 = ((s32[32,4,128]{2,1,0:T(4,128)}), s32[32,4,128]{2,1,0:T(4,128)S(1)}, u32[]{:S(2)}, u32[]{:S(2)}) async-start(s32[32,4,128]{2,1,0:T(4,128)} %bitcast.13), calls=%async_computation.1 | async-start | bytes 131072 | tf_op jit(solution)/shard_map/all_to_all | solution.py:575
  22.5 0.0 copy-done
  22.6 27.5 %score.1.scores_ref = f32[1024,128]{1,0:T(8,128)} custom-call(bf16[1024,128]{1,0:T(8,128)(2,1)} %bitcast.8, bf16[1024,1024]{1,0:T(8,128)(2,1)} %items_hbm.1, bf16[256,256]{1,0:T(8,128)(2,1)} %get-tuple-element.10.gate_ref, bf16[256,128]{1,0:T(8,128)(2,1)} %get-tuple-element.11.bias_ref), custom_call_target="tpu_custom_call" | custom-call | tf_op jit(solution)/shard_map/score/pallas_call | solution.py:202
  50.0 0.0 all-to-all-done.1
  50.1 0.0 copy-start.1
  50.1 0.6 copy-done.1
  50.7 23.2 %rank.1 = f32[128,128]{1,0:T(8,128)} custom-call(f32[1024,128]{1,0:T(8,128)} %score.1.scores_ref, bf16[1024,128]{1,0:T(8,128)(2,1)} %bitcast.9, s32[128,128]{1,0:T(8,128)} %bitcast.10, bf16[1024,1024]{1,0:T(8,128)(2,1)} %items_hbm.1, bf16[3,1024,1024]{2,1,0:T(8,128)(2,1)} %weight_hbm.1, f32[3,1024]{1,0:T(4,128)} %bias_ref.1, f32[1,1024]{1,0:T(1,128)} %bitcast.16), custom_call_target="tpu_custom_call" | custom-call | tf_op jit(solution)/shard_map/rank/pallas_call | solution.py:449
  73.9 13.4 %all_to_all.27 = f32[32,4,128]{2,1,0:T(4,128)} all-to-all(f32[32,4,128]{2,1,0:T(4,128)} %bitcast.11), channel_id=1, replica_groups=mesh['groups'=1,'cand'=32] {'cand'}, dimensions={0} | all-to-all | bytes 131072 | tf_op jit(solution)/shard_map/all_to_all | solution.py:575
  87.2 3.1 %merge.1 = (f32[4,96]{1,0:T(4,128)}, f32[768]{0:T(1024)}) custom-call(f32[128,128]{1,0:T(8,128)} %bitcast.12, s32[1,768]{1,0:T(1,128)} %bitcast.15, s32[1,768]{1,0:T(1,128)} %get-tuple-element.13.place_ref), custom_call_target="tpu_custom_call" | custom-call | tf_op jit(solution)/shard_map/merge/pallas_call | solution.py:558
Async XLA Ops:
  2.1 17.9 %all-to-all-start = ((bf16[32,32,128]{2,1,0:T(8,128)(2,1)}), bf16[32,32,128]{2,1,0:T(8,128)(2,1)S(1)}, u32[]{:S(2)}, u32[]{:S(2)}) async-start(bf16[32,32,128]{2,1,0:T(8,128)(2,1)} %broadcast_in_dim.8), calls=%async_computation | async-start | bytes 524288 | tf_op jit(solution)/shard_map/all_to_all | solution.py:575
  20.0 2.6 %copy-start = (bf16[32,32,128]{2,1,0:T(8,128)(2,1)}, bf16[32,32,128]{2,1,0:T(8,128)(2,1)S(1)}, u32[]{:S(2)}) copy-start(bf16[32,32,128]{2,1,0:T(8,128)(2,1)S(1)} %all-to-all-done) | copy-start | bytes 786436
  20.0 30.1 %all-to-all-start.1 = ((s32[32,4,128]{2,1,0:T(4,128)}), s32[32,4,128]{2,1,0:T(4,128)S(1)}, u32[]{:S(2)}, u32[]{:S(2)}) async-start(s32[32,4,128]{2,1,0:T(4,128)} %bitcast.13), calls=%async_computation.1 | async-start | bytes 131072 | tf_op jit(solution)/shard_map/all_to_all | solution.py:575
  50.1 0.6 copy-start.1

commit v2 on v1

--- a/solution.py
+++ b/solution.py
@@ -18,10 +18,14 @@
 LANES = 128
 SUBLANES = 4
 BLOCKS = 2
+SORT_AT = 0
 COLUMNS = 256
 NEVER = -1e30
 TILE_COLS = 256
 GROUP = 4
+UNROLL = 32
+AHEAD = 8
+ROWS = 512
 BASE = 32
 LOG2E = math.log2(math.e)
 SCALE = 1.0 / math.sqrt(D)
@@ -98,12 +102,12 @@
     side = GROUP * PAIRS
     step = GROUP * EMB
     row, col = iota((side, PAIRS), 0), iota((side, PAIRS), 1)
-    select = ones_where((row % EMB) * EMB + row // step == col)
+    select = ones_where((row % step // GROUP) * EMB + row // step == col)
     part = dot_nt(select, gate_ref[...]).astype(BF16)
     full = dot_nt(part, select)
-    same = (iota((side, side), 0) // EMB) % GROUP == (iota((side, side), 1) // EMB) % GROUP
+    same = iota((side, side), 0) % GROUP == iota((side, side), 1) % GROUP
     gate_out[...] = jnp.where(same, full, 0.0).astype(BF16)
-    order = (row % EMB) * EMB + row // step == col
+    order = (row % step // GROUP) * EMB + row // step == col
     column = jnp.sum(jnp.where(order, bias_ref[...], 0.0), axis=1, keepdims=True)
     bias_out[...] = jnp.broadcast_to(column, bias_out.shape).astype(BF16)
 
@@ -124,30 +128,39 @@
 
 
 def score_kernel(query_ref, items_ref, gate_ref, bias_ref, scores_ref,
-                 dots_a, dots_b, num_ref, den_ref, *logits):
+                 dots_ref, num_ref, den_ref, *logits):
     query_rows = query_ref.shape[0]
     tiles = items_ref.shape[0] // TILE_COLS
     step = GROUP * EMB
     groups = query_rows // step
-    row_blocks = query_rows // TILE_COLS
-
-    def piece(tile, index, out):
-        j, block = index // row_blocks, index % row_blocks
-        start = pl.multiple_of(block * TILE_COLS, TILE_COLS)
-        lanes = pl.multiple_of(j * D, D)
-        values = dot_nt(
-            query_ref[pl.ds(start, TILE_COLS), :],
-            items_ref[tile * TILE_COLS : (tile + 1) * TILE_COLS, pl.ds(lanes, D)],
-        )
-        out[j, pl.ds(start, TILE_COLS), :] = (values * SCALE).astype(BF16)
-
-    def gate(dots, group, out):
-        start = pl.multiple_of(group * step, step)
-        part = dots[:, pl.ds(start, step), :].reshape(GROUP * PAIRS, TILE_COLS)
+    units = tiles * groups
+
+    @pl.loop(0, tiles * EMB // AHEAD)
+    def _(index):
+        for k in range(AHEAD):
+            piece = index * AHEAD + k
+            tile, j = piece // EMB, piece % EMB
+            start = pl.multiple_of(tile * TILE_COLS, TILE_COLS)
+            lanes = pl.multiple_of(j * D, D)
+            for block in range(query_rows // ROWS):
+                rows = slice(block * ROWS, (block + 1) * ROWS)
+                values = dot_nt(
+                    query_ref[rows, :], items_ref[pl.ds(start, TILE_COLS), pl.ds(lanes, D)]
+                )
+                dots_ref[tile, j, rows, :] = (values * SCALE).astype(BF16)
+
+    def place(unit):
+        unit = jnp.minimum(unit, units - 1)
+        tile, group = unit // groups, unit % groups
+        return tile, pl.multiple_of(group * step, step), group
+
+    def gate(unit, out):
+        tile, start, _ = place(unit)
+        part = dots_ref[tile, :, pl.ds(start, step), :].reshape(GROUP * PAIRS, TILE_COLS)
         out[...] = dot(gate_ref[...], part).astype(BF16)
 
-    def mix(dots, group, logits):
-        start = pl.multiple_of(group * step, step)
+    def mix(unit, logits):
+        tile, start, _ = place(unit)
         weights, products = [], []
         for j in range(EMB):
             bias = bias_ref[j * step : (j + 1) * step, :]
@@ -155,58 +168,48 @@
             power = jnp.exp2(jnp.minimum(logit * LOG2E, 126.0))
             weight = jnp.maximum(jnp.log(1.0 + power), logit)
             weights.append(weight)
-            products.append(weight * dots[j, pl.ds(start, step), :])
-        den = tree_sum(weights)
-        num = tree_sum(products)
-        for half in range(TILE_COLS // LANES):
-            lanes = slice(half * LANES, (half + 1) * LANES)
-            num_ref[half, pl.ds(start, step), :] = num[:, lanes]
-            den_ref[half, pl.ds(start, step), :] = den[:, lanes]
-
-    buffers = (dots_a, dots_b)
-
-    @pl.loop(0, groups)
+            products.append(weight * dots_ref[tile, j, pl.ds(start, step), :])
+        totals = []
+        for values in (weights, products):
+            both = jnp.sum(tree_sum(values).reshape(step // (2 * GROUP), 2 * GROUP, TILE_COLS), axis=0)
+            totals.append(both + pltpu.roll(both, GROUP, 0))
+        return totals
+
+    def keep(unit, even, odd):
+        tile, _, group = place(unit)
+        rows = pl.ds(pl.multiple_of(group * GROUP, 2 * GROUP), 2 * GROUP)
+        upper = iota((2 * GROUP, TILE_COLS), 0) < GROUP
+        for out, a, b in zip((den_ref, num_ref), even, odd):
+            out[tile, rows, :] = jnp.where(upper, a, b)
+
+    gate(0, logits[0])
+    gate(1, logits[1])
+
+    @pl.loop(0, units // UNROLL)
     def _(index):
-        piece(0, index, dots_a)
+        for phase in range(UNROLL // 2):
+            first = index * UNROLL + phase * 2
+            side = 2 * (phase % 2)
+            here, there = logits[side : side + 2], logits[2 - side : 4 - side]
+            for k in range(2):
+                gate(first + 2 + k, there[k])
+            keep(first, mix(first, here[0]), mix(first + 1, here[1]))
 
     for tile in range(tiles):
-        dots, ahead = buffers[tile % 2], buffers[(tile + 1) % 2]
-        gate(dots, 0, logits[0])
-        gate(dots, 1, logits[1])
-
-        @pl.loop(0, groups // 8)
-        def _(quad):
-            for phase in range(4):
-                first = quad * 8 + phase * 2
-                here, there = logits[2 * (phase % 2) : 2 * (phase % 2) + 2], logits[2 - 2 * (phase % 2) : 4 - 2 * (phase % 2)]
-                if tile + 1 < tiles:
-                    piece(tile + 1, first, ahead)
-                    piece(tile + 1, first + 1, ahead)
-                for k in range(2):
-                    gate(dots, jnp.minimum(first + 2 + k, groups - 1), there[k])
-                for k in range(2):
-                    mix(dots, first + k, here[k])
-
-        for half in range(TILE_COLS // LANES):
-            num = jnp.zeros((query_rows // EMB, LANES), F32)
-            den = jnp.ones((query_rows // EMB, LANES), F32)
-            for i in range(EMB):
-                num = num + num_ref[half, pl.ds(i, query_rows // EMB, stride=EMB), :]
-                den = den + den_ref[half, pl.ds(i, query_rows // EMB, stride=EMB), :]
-            start = tile * TILE_COLS + half * LANES
-            scores_ref[start : start + LANES, :] = (num / den).T
+        values = num_ref[tile] / (1.0 + den_ref[tile])
+        scores_ref[tile * TILE_COLS : (tile + 1) * TILE_COLS, :] = values.T
 
 
 def score(queries, items, gate_full, bias_full):
     query_rows, item_rows = queries.shape[0], items.shape[0]
+    tiles = item_rows // TILE_COLS
     return pl.pallas_call(
         score_kernel,
         out_shape=jax.ShapeDtypeStruct((item_rows, query_rows // EMB), F32),
         scratch_shapes=[
-            pltpu.VMEM((EMB, query_rows, TILE_COLS), BF16),
-            pltpu.VMEM((EMB, query_rows, TILE_COLS), BF16),
-            pltpu.VMEM((TILE_COLS // LANES, query_rows, LANES), F32),
-            pltpu.VMEM((TILE_COLS // LANES, query_rows, LANES), F32),
+            pltpu.VMEM((tiles, EMB, query_rows, TILE_COLS), BF16),
+            pltpu.VMEM((tiles, query_rows // EMB, TILE_COLS), F32),
+            pltpu.VMEM((tiles, query_rows // EMB, TILE_COLS), F32),
         ]
         + [pltpu.VMEM((GROUP * PAIRS, TILE_COLS), BF16) for _ in range(4)],
         compiler_params=pltpu.CompilerParams(vmem_limit_bytes=VMEM),
@@ -302,7 +305,7 @@
 
 
 def rank_kernel(scores_ref, query_ref, codes_ref, items_hbm, weight_hbm, bias_ref, out_weight_ref,
-                result_ref, weight_ref, table_ref, query_f32, pair_ref, sort_a, sort_b, best_ref,
+                result_ref, weight_ref, table_ref, query_f32, user_f32, pair_ref, sort_a, sort_b, best_ref,
                 pick_ref, first_ref, state_ref, round_a, round_b, weight_sem, items_sem, *, fetch):
     item_rows, requests = scores_ref.shape
     weight_copy = pltpu.make_async_copy(weight_hbm, weight_ref, weight_sem)
@@ -314,13 +317,13 @@
 
     query_f32[...] = query_ref[...].astype(F32)
     for i in range(EMB):
-        users = query_f32[pl.ds(i, requests, stride=EMB), :].astype(BF16)
-        table_ref[item_rows:, i * D : (i + 1) * D] = users
+        for r in range(local):
+            rows = query_f32[pl.ds(i * local + r, size, stride=local * EMB), :]
+            user_f32[i, pl.ds(r, size, stride=local), :] = rows
+        table_ref[item_rows:, i * D : (i + 1) * D] = user_f32[i].astype(BF16)
     pair_ref[:, :requests], pair_ref[:, requests:] = split_two(scores_ref[...])
     items_copy.wait()
     weight_copy.wait()
-    best_of(scores_ref, codes_ref, result_ref, sort_a, sort_b, best_ref, local)
-
     total = size * fetch
     block = total // BLOCKS
     width = first_ref.shape[-1]
@@ -329,19 +332,21 @@
         [code_item // BASE, code_item % BASE, codes_ref[message(1, size), :]], axis=1
     ).astype(F32).astype(BF16)
     answer = jnp.zeros((size, LANES), F32)
+
+    def source_of(shape, dim, start):
+        row = (iota(shape, dim) + start).astype(F32)
+        return jnp.floor((row + 0.5) * (1.0 / fetch))
+
+    def slot_of(start):
+        source = source_of((block, LANES), 0, start).astype(jnp.int32)
+        return iota((block, LANES), 0) + start - source * fetch == iota((block, LANES), 1)
+
     for part in range(BLOCKS):
         start = part * block
-        pick, first, state = pick_ref.at[part], first_ref.at[part], state_ref.at[part]
-        rounded = (round_a.at[part], round_b.at[part])
-
-        def source_of(shape, dim):
-            row = (iota(shape, dim) + start).astype(F32)
-            return jnp.floor((row + 0.5) * (1.0 / fetch))
-
-        from_source = ones_where(source_of((block, size), 0) == iota((block, size), 1).astype(F32))
-        taken = dot(from_source, digits)
-        slot = iota((block, LANES), 0) + start - source_of((block, LANES), 0).astype(jnp.int32) * fetch
-        mine = slot == iota((block, LANES), 1)
+        pick = pick_ref.at[part]
+        from_source = source_of((block, size), 0, start) == iota((block, size), 1).astype(F32)
+        taken = dot(ones_where(from_source), digits)
+        mine = slot_of(start)
         item = jnp.sum(
             jnp.where(mine, taken[:, :LANES] * BASE + taken[:, LANES : 2 * LANES], 0.0),
             axis=1, keepdims=True,
@@ -349,38 +354,49 @@
         request = jnp.sum(
             jnp.where(mine, taken[:, 2 * LANES :], 0.0), axis=1, keepdims=True
         ).astype(jnp.int32)
-        asked = request == iota((block, requests), 1)
         pick[:, :item_rows] = ones_where(item == iota((block, item_rows), 1))
-        pick[:, item_rows:] = ones_where(asked)
-        mixed = dot(pick[:, :item_rows], pair_ref[...])
-        mixed = jnp.where(asked, mixed[:, :requests] + mixed[:, requests:], 0.0)
-        partial = mixed[:, :LANES]
-        for i in range(1, requests // LANES):
-            partial = partial + mixed[:, i * LANES : (i + 1) * LANES]
-
+        pick[:, item_rows:] = ones_where(request == iota((block, requests), 1))
+
+    layers = weight_ref.shape[0]
+    for part in range(BLOCKS):
         for column in range(0, width, COLUMNS):
             columns = slice(column, column + COLUMNS)
-            values = dot(pick[...], table_ref[:, columns])
-            first[:, columns] = values
-            rounded[0][:, columns] = values.astype(BF16)
-        layers = weight_ref.shape[0]
-        for layer in range(layers):
+            values = dot(pick_ref[part], table_ref[:, columns])
+            first_ref[part, :, columns] = values
+            round_a[part, :, columns] = values.astype(BF16)
+    partial = [None] * BLOCKS
+    rounded = (round_a, round_b)
+    for layer in range(layers):
+        for part in range(BLOCKS):
             for column in range(0, width, COLUMNS):
                 columns = slice(column, column + COLUMNS)
-                hidden = dot(rounded[layer % 2][...], weight_ref[layer, :, columns])
+                hidden = dot(rounded[layer % 2][part], weight_ref[layer, :, columns])
                 hidden = hidden + bias_ref[layer : layer + 1, columns]
-                before = (state if layer else first)[:, columns]
-                after = first[:, columns] * hidden + before
+                first = first_ref[part, :, columns]
+                after = first * hidden + (state_ref[part, :, columns] if layer else first)
                 if layer + 1 < layers:
-                    state[:, columns] = after
-                    rounded[(layer + 1) % 2][:, columns] = after.astype(BF16)
+                    state_ref[part, :, columns] = after
+                    rounded[(layer + 1) % 2][part, :, columns] = after.astype(BF16)
                 else:
                     weighted = after * out_weight_ref[:, columns]
                     for i in range(COLUMNS // LANES):
-                        partial = partial + weighted[:, i * LANES : (i + 1) * LANES]
-        column = jnp.sum(partial, axis=1, keepdims=True)
-        placed = jnp.where(mine, column, 0.0)
-        to_source = ones_where(source_of((size, block), 1) == iota((size, block), 0).astype(F32))
+                        term = weighted[:, i * LANES : (i + 1) * LANES]
+                        partial[part] = term if partial[part] is None else partial[part] + term
+        if layer == SORT_AT:
+            best_of(scores_ref, codes_ref, result_ref, sort_a, sort_b, best_ref, local)
+    for part in range(BLOCKS):
+        start = part * block
+        mixed = dot(pick_ref[part, :, :item_rows], pair_ref[...])
+        mixed = mixed[:, :requests] + mixed[:, requests:]
+        mixed = mixed * pick_ref[part, :, item_rows:].astype(F32)
+        total_row = partial[part]
+        for i in range(requests // LANES):
+            total_row = total_row + mixed[:, i * LANES : (i + 1) * LANES]
+        column = jnp.sum(total_row, axis=1, keepdims=True)
+        placed = jnp.where(slot_of(start), column, 0.0)
+        to_source = ones_where(
+            source_of((size, block), 1, start) == iota((size, block), 0).astype(F32)
+        )
         high, rest = split_two(placed)
         middle, low = split_two(placed - high.astype(F32))
         answer = answer + (dot(to_source, high) + (dot(to_source, middle) + dot(to_source, low)))
@@ -455,6 +471,7 @@
             pltpu.VMEM(cross_weight.shape, BF16),
             pltpu.VMEM((item_rows + requests, width), BF16),
             pltpu.VMEM(queries.shape, F32),
+            pltpu.VMEM((EMB, requests, D), F32),
             pltpu.VMEM((item_rows, 2 * requests), BF16),
             pltpu.VMEM((item_rows // EMB, EMB, LANES), F32),
             pltpu.VMEM((item_rows // EMB, EMB, LANES), F32),
@@ -581,7 +598,7 @@
     local = users.shape[0]
     rows = row_item.shape[0]
     fetch = max(2, 2 * rows // size)
-    own = users.reshape(1, local * EMB, D)
+    own = users.reshape(local, EMB, D).swapaxes(0, 1).reshape(1, local * EMB, D)
     queries = exchange(jnp.broadcast_to(own, (size, local * EMB, D)))
     queries = queries.reshape(size * local * EMB, D)
     owner = row_device.reshape(1, rows)

time: 90.9 us -> 84.7 us (0.932)
  Pallas kernels: 55.7 us -> 49.5 us
    pallas_call x1, Pallas kernels: 27.5 us -> 21.3 us  [score(): pl.pallas_call(score_kernel, out_shape=jax.ShapeDtypeStruct((item_rows, q...]
  transfers between devices with their start and end apart: 2 -> 2, of which waited for: 1 -> 1; matrix products, arithmetic and copies ran while one was open for 3% -> 3% of each run, Pallas kernels for 33% -> 28%
where the time goes in v2:
time: 84.7 us; the launch traced here: 84.1 us
  Pallas kernels  49.5 us (58%)
  blocking collectives  13.4 us (16%)
  starting transfers between devices  9.86 us (12%)
  waiting for transfers between devices  6.13 us (7%)
  local copies, waits for them, and re-layouts  4.62 us (5%)
    pallas_call x1, Pallas kernels, rank(): pl.pallas_call(functools.partial(rank_kernel, fetch=fetch), out_shape=jax...  23.1 us
    pallas_call x1, Pallas kernels, score(): pl.pallas_call(score_kernel, out_shape=jax.ShapeDtypeStruct((item_rows, q...  21.3 us
    all_to_all x1, blocking collectives, exchange(): return lax.all_to_all(x, 'cand', split_axis=0, concat_axis=0, tiled=True)  13.4 us
    all_to_all x2, starting transfers between devices, exchange(): return lax.all_to_all(x, 'cand', split_axis=0, concat_axis=0, tiled=True)  9.86 us
    all_to_all x2, waiting for transfers between devices, exchange(): return lax.all_to_all(x, 'cand', split_axis=0, concat_axis=0, tiled=True)  6.13 us
    pallas_call x1, Pallas kernels, merge(): pl.pallas_call(merge_kernel, out_shape=(jax.ShapeDtypeStruct((local, KEEP...  3.15 us
    pallas_call x1, Pallas kernels, plan(): pl.pallas_call(plan_kernel, out_shape=(jax.ShapeDtypeStruct((size * SUBLA...  1.92 us
  transfers between devices with their start and end apart: 2, of which 1 were waited for; matrix products, arithmetic and copies ran while one was open for 3% of the time, Pallas kernels for 28%

profile of v2, /device:TPU:0, one launch (start us, length us, event | category | flops | bytes accessed | tf_op | source)
XLA Modules:
  0.0 84.1 jit_solution(11074533048052871465)
XLA Ops:
  0.6 1.4 %broadcast_in_dim.8 = bf16[32,32,128]{2,1,0:T(8,128)(2,1)} broadcast(bf16[32,128]{1,0:T(8,128)(2,1)} %bitcast.21), dimensions={1,2} | broadcast | bytes 270336 | tf_op jit(solution)/shard_map/broadcast_in_dim | solution.py:602
  2.1 7.3 %all-to-all-start = ((bf16[32,32,128]{2,1,0:T(8,128)(2,1)}), bf16[32,32,128]{2,1,0:T(8,128)(2,1)S(1)}, u32[]{:S(2)}, u32[]{:S(2)}) async-start(bf16[32,32,128]{2,1,0:T(8,128)(2,1)} %broadcast_in_dim.8), calls=%async_computation | async-start | bytes 524288 | tf_op jit(solution)/shard_map/all_to_all | solution.py:592
  9.4 1.3 %reshape.34.item_ref = s32[1,768]{1,0:T(1,128)} reshape(s32[768]{0:T(1024)} %param.20) | data formatting | bytes 6144 | tf_op jit(solution)/shard_map/reshape | solution.py:606
  10.6 1.3 %reshape.35.request_ref = s32[1,768]{1,0:T(1,128)} reshape(s32[768]{0:T(1024)} %param.21) | data formatting | bytes 6144 | tf_op jit(solution)/shard_map/reshape | solution.py:606
  11.9 1.9 %plan.1 = (s32[128,128]{1,0:T(8,128)}, s32[1,768]{1,0:T(1,128)}, bf16[256,256]{1,0:T(8,128)(2,1)}, bf16[256,128]{1,0:T(8,128)(2,1)}) custom-call(s32[1,768]{1,0:T(1,128)} %bitcast.19, s32[1,768]{1,0:T(1,128)} %reshape.34.item_ref, s32[1,768]{1,0:T(1,128)} %reshape.35.request_ref, s32[4,32]{1,0:T(4,128)} %probes_ref.1, bf16[64,64]{1,0:T(8,128)(2,1)} %gate_ref.1, ...), custom_call_target="tpu_custom_call" | custom-call | tf_op jit(solution)/shard_map/plan/pallas_call | solution.py:117
  13.8 6.1 %all-to-all-done = bf16[32,32,128]{2,1,0:T(8,128)(2,1)S(1)} async-done(((bf16[32,32,128]{2,1,0:T(8,128)(2,1)}), bf16[32,32,128]{2,1,0:T(8,128)(2,1)S(1)}, u32[]{:S(2)}, u32[]{:S(2)}) %all-to-all-start) | async-done | bytes 262176 | tf_op jit(solution)/shard_map/all_to_all | solution.py:592
  20.0 0.0 copy-start
  20.0 2.6 %all-to-all-start.1 = ((s32[32,4,128]{2,1,0:T(4,128)}), s32[32,4,128]{2,1,0:T(4,128)S(1)}, u32[]{:S(2)}, u32[]{:S(2)}) async-start(s32[32,4,128]{2,1,0:T(4,128)} %bitcast.18), calls=%async_computation.1 | async-start | bytes 131072 | tf_op jit(solution)/shard_map/all_to_all | solution.py:592
  22.5 0.0 copy-done
  22.5 21.3 %score.1.scores_ref = f32[1024,128]{1,0:T(8,128)} custom-call(bf16[1024,128]{1,0:T(8,128)(2,1)} %bitcast.13, bf16[1024,1024]{1,0:T(8,128)(2,1)} %items_hbm.1, bf16[256,256]{1,0:T(8,128)(2,1)} %get-tuple-element.10.gate_ref, bf16[256,128]{1,0:T(8,128)(2,1)} %get-tuple-element.11.bias_ref), custom_call_target="tpu_custom_call" | custom-call | tf_op jit(solution)/shard_map/score/pallas_call | solution.py:206
  43.8 0.0 all-to-all-done.1
  43.8 0.0 copy-start.1
  43.8 0.6 copy-done.1
  44.5 23.1 %rank.1 = f32[128,128]{1,0:T(8,128)} custom-call(f32[1024,128]{1,0:T(8,128)} %score.1.scores_ref, bf16[1024,128]{1,0:T(8,128)(2,1)} %bitcast.14, s32[128,128]{1,0:T(8,128)} %bitcast.15, bf16[1024,1024]{1,0:T(8,128)(2,1)} %items_hbm.1, bf16[3,1024,1024]{2,1,0:T(8,128)(2,1)} %weight_hbm.1, f32[3,1024]{1,0:T(4,128)} %bias_ref.1, f32[1,1024]{1,0:T(1,128)} %bitcast.22), custom_call_target="tpu_custom_call" | custom-call | tf_op jit(solution)/shard_map/rank/pallas_call | solution.py:465
  67.6 13.4 %all_to_all.27 = f32[32,4,128]{2,1,0:T(4,128)} all-to-all(f32[32,4,128]{2,1,0:T(4,128)} %bitcast.16), channel_id=1, replica_groups=mesh['groups'=1,'cand'=32] {'cand'}, dimensions={0} | all-to-all | bytes 131072 | tf_op jit(solution)/shard_map/all_to_all | solution.py:592
  81.0 3.1 %merge.1 = (f32[4,96]{1,0:T(4,128)}, f32[768]{0:T(1024)}) custom-call(f32[128,128]{1,0:T(8,128)} %bitcast.17, s32[1,768]{1,0:T(1,128)} %bitcast.20, s32[1,768]{1,0:T(1,128)} %get-tuple-element.13.place_ref), custom_call_target="tpu_custom_call" | custom-call | tf_op jit(solution)/shard_map/merge/pallas_call | solution.py:575
Async XLA Ops:
  2.1 17.9 %all-to-all-start = ((bf16[32,32,128]{2,1,0:T(8,128)(2,1)}), bf16[32,32,128]{2,1,0:T(8,128)(2,1)S(1)}, u32[]{:S(2)}, u32[]{:S(2)}) async-start(bf16[32,32,128]{2,1,0:T(8,128)(2,1)} %broadcast_in_dim.8), calls=%async_computation | async-start | bytes 524288 | tf_op jit(solution)/shard_map/all_to_all | solution.py:592
  20.0 2.6 %copy-start = (bf16[32,32,128]{2,1,0:T(8,128)(2,1)}, bf16[32,32,128]{2,1,0:T(8,128)(2,1)S(1)}, u32[]{:S(2)}) copy-start(bf16[32,32,128]{2,1,0:T(8,128)(2,1)S(1)} %all-to-all-done) | copy-start | bytes 786436
  20.0 23.9 %all-to-all-start.1 = ((s32[32,4,128]{2,1,0:T(4,128)}), s32[32,4,128]{2,1,0:T(4,128)S(1)}, u32[]{:S(2)}, u32[]{:S(2)}) async-start(s32[32,4,128]{2,1,0:T(4,128)} %bitcast.18), calls=%async_computation.1 | async-start | bytes 131072 | tf_op jit(solution)/shard_map/all_to_all | solution.py:592
  43.8 0.6 copy-start.1

commit v3 on v2

--- a/solution.py
+++ b/solution.py
@@ -322,8 +322,6 @@
             user_f32[i, pl.ds(r, size, stride=local), :] = rows
         table_ref[item_rows:, i * D : (i + 1) * D] = user_f32[i].astype(BF16)
     pair_ref[:, :requests], pair_ref[:, requests:] = split_two(scores_ref[...])
-    items_copy.wait()
-    weight_copy.wait()
     total = size * fetch
     block = total // BLOCKS
     width = first_ref.shape[-1]
@@ -358,6 +356,7 @@
         pick[:, item_rows:] = ones_where(request == iota((block, requests), 1))
 
     layers = weight_ref.shape[0]
+    items_copy.wait()
     for part in range(BLOCKS):
         for column in range(0, width, COLUMNS):
             columns = slice(column, column + COLUMNS)
@@ -366,6 +365,7 @@
             round_a[part, :, columns] = values.astype(BF16)
     partial = [None] * BLOCKS
     rounded = (round_a, round_b)
+    weight_copy.wait()
     for layer in range(layers):
         for part in range(BLOCKS):
             for column in range(0, width, COLUMNS):
@@ -489,7 +489,7 @@
     )(scores, queries, codes, items, cross_weight, cross_bias, out_weight)
 
 
-def merge_kernel(back_ref, owner_ref, place_ref, top_ref, rerank_ref, list_ref, merge_a, merge_b):
+def merge_kernel(back_ref, owner_ref, place_ref, top_ref, rerank_ref, list_ref):
     size = back_ref.shape[0] // SUBLANES
     local = top_ref.shape[0]
     rows = owner_ref.shape[1]
@@ -509,65 +509,36 @@
     for r in range(local):
         best = back_ref[message(r, size), :]
         list_ref[pl.ds(r, size, stride=local), :] = jnp.where(iota(best.shape, 1) < KEEP, best, NEVER)
-    chunks = size * local // LANES
-    merge_a[...] = list_ref[...].T
-
-    def reader(ref, chunk=0):
-        return lambda i: ref[i : i + 1, chunk * LANES : (chunk + 1) * LANES]
-
-    def writer(ref):
-        def store(i, value):
-            ref[i : i + 1, :LANES] = value
-        return store
-
-    held, other = merge_a, merge_b
-    while chunks > 1:
-        half = chunks // 2
-        for chunk in range(half):
-            take = slice(chunk * LANES, (chunk + 1) * LANES)
-
-            def load(i, ref=held, first=chunk, second=chunk + half):
-                return ref[i : i + 1, first * LANES : (first + 1) * LANES]
-
-            def store(i, value, ref=other, take=take):
-                ref[i : i + 1, take] = value
-
-            def read(i, ref=other, take=take):
-                return ref[i : i + 1, take]
-
-            merge_pairs(
-                load,
-                lambda i, ref=held, c=chunk + half: ref[i : i + 1, c * LANES : (c + 1) * LANES],
-                store, read, LANES,
-            )
-        held, other = other, held
-        chunks = half
+    lists = list_ref[...].T
+    while lists.shape[1] > LANES:
+        half = lists.shape[1] // 2
+        lists = best_of_two(lists[:, :half], lists[:, half:])
     shift = LANES // 2
     while shift >= local:
-        merge_top(
-            reader(held), writer(other), reader(other),
-            functools.partial(pltpu.roll, shift=LANES - shift, axis=1), LANES,
-        )
-        held, other = other, held
+        lists = best_of_two(lists, pltpu.roll(lists, LANES - shift, 1))
         shift //= 2
-    top_ref[...] = held[:, :LANES].T[:local, :KEEP]
-
-
-def merge_pairs(load, load_other, store, load_merged, total):
-    for i in range(total):
-        store(i, jnp.maximum(load(i), load_other(total - 1 - i)))
-    quarter = total // 4
-    for i in range(quarter):
-        spots = [i, i + quarter, i + 2 * quarter, i + 3 * quarter]
-        values = [load_merged(spot) for spot in spots]
-        order_pair(values, 0, 2)
-        order_pair(values, 1, 3)
-        order_pair(values, 0, 1)
-        order_pair(values, 2, 3)
-        for spot, value in zip(spots, values):
-            store(spot, value)
-    for offset in range(0, total, quarter):
-        clean_block(load_merged, store, offset, quarter)
+    top_ref[...] = lists.T[:local, :KEEP]
+
+
+def neighbour(x, distance):
+    upper = (iota(x.shape, 0) & distance) == 0
+    return jnp.where(upper, pltpu.roll(x, EMB - distance, 0), pltpu.roll(x, distance, 0)), upper
+
+
+def best_of_two(a, b):
+    count = a.shape[0] // EMB
+    values = []
+    for i in range(count):
+        other = b[(count - 1 - i) * EMB : (count - i) * EMB, :]
+        for distance in (1, 2, 4):
+            other = neighbour(other, distance)[0]
+        values.append(jnp.maximum(a[i * EMB : (i + 1) * EMB, :], other))
+    clean(values)
+    for distance in (4, 2, 1):
+        for i, value in enumerate(values):
+            other, upper = neighbour(value, distance)
+            values[i] = jnp.where(upper, jnp.maximum(value, other), jnp.minimum(value, other))
+    return jnp.concatenate(values, axis=0)
 
 
 def merge(back, owner, place, local):
@@ -580,8 +551,6 @@
         ),
         scratch_shapes=[
             pltpu.VMEM((size * local, LANES), F32),
-            pltpu.VMEM((LANES, size * local), F32),
-            pltpu.VMEM((LANES, size * local), F32),
         ],
         compiler_params=pltpu.CompilerParams(vmem_limit_bytes=VMEM),
         name="merge",

time: 84.7 us -> 81.6 us (0.963)
  Pallas kernels: 49.5 us -> 46.4 us
    pallas_call x1, Pallas kernels: 23.1 us -> 21 us  [rank(): pl.pallas_call(functools.partial(rank_kernel, fetch=fetch), out_shape=jax...]
    pallas_call x1, Pallas kernels: 3.15 us -> 2.21 us  [merge(): pl.pallas_call(merge_kernel, out_shape=(jax.ShapeDtypeStruct((local, KEEP...]
  transfers between devices with their start and end apart: 2 -> 2, of which waited for: 1 -> 1; matrix products, arithmetic and copies ran while one was open for 3% -> 3% of each run, Pallas kernels for 28% -> 29%
where the time goes in v3:
time: 81.6 us; the launch traced here: 81 us
  Pallas kernels  46.4 us (57%)
  blocking collectives  13.4 us (16%)
  starting transfers between devices  9.86 us (12%)
  waiting for transfers between devices  6.13 us (8%)
  local copies, waits for them, and re-layouts  4.62 us (6%)
    pallas_call x1, Pallas kernels, score(): pl.pallas_call(score_kernel, out_shape=jax.ShapeDtypeStruct((item_rows, q...  21.3 us
    pallas_call x1, Pallas kernels, rank(): pl.pallas_call(functools.partial(rank_kernel, fetch=fetch), out_shape=jax...  21 us
    all_to_all x1, blocking collectives, exchange(): return lax.all_to_all(x, 'cand', split_axis=0, concat_axis=0, tiled=True)  13.4 us
    all_to_all x2, starting transfers between devices, exchange(): return lax.all_to_all(x, 'cand', split_axis=0, concat_axis=0, tiled=True)  9.86 us
    all_to_all x2, waiting for transfers between devices, exchange(): return lax.all_to_all(x, 'cand', split_axis=0, concat_axis=0, tiled=True)  6.13 us
    pallas_call x1, Pallas kernels, merge(): pl.pallas_call(merge_kernel, out_shape=(jax.ShapeDtypeStruct((local, KEEP...  2.21 us
    pallas_call x1, Pallas kernels, plan(): pl.pallas_call(plan_kernel, out_shape=(jax.ShapeDtypeStruct((size * SUBLA...  1.92 us
  transfers between devices with their start and end apart: 2, of which 1 were waited for; matrix products, arithmetic and copies ran while one was open for 3% of the time, Pallas kernels for 29%

profile of v3, /device:TPU:0, one launch (start us, length us, event | category | flops | bytes accessed | tf_op | source)
XLA Modules:
  0.0 81.0 jit_solution(11155436997672800068)
XLA Ops:
  0.6 1.4 %broadcast_in_dim.8 = bf16[32,32,128]{2,1,0:T(8,128)(2,1)} broadcast(bf16[32,128]{1,0:T(8,128)(2,1)} %bitcast.21), dimensions={1,2} | broadcast | bytes 270336 | tf_op jit(solution)/shard_map/broadcast_in_dim | solution.py:571
  2.1 7.3 %all-to-all-start = ((bf16[32,32,128]{2,1,0:T(8,128)(2,1)}), bf16[32,32,128]{2,1,0:T(8,128)(2,1)S(1)}, u32[]{:S(2)}, u32[]{:S(2)}) async-start(bf16[32,32,128]{2,1,0:T(8,128)(2,1)} %broadcast_in_dim.8), calls=%async_computation | async-start | bytes 524288 | tf_op jit(solution)/shard_map/all_to_all | solution.py:561
  9.4 1.3 %reshape.34.item_ref = s32[1,768]{1,0:T(1,128)} reshape(s32[768]{0:T(1024)} %param.20) | data formatting | bytes 6144 | tf_op jit(solution)/shard_map/reshape | solution.py:575
  10.6 1.3 %reshape.35.request_ref = s32[1,768]{1,0:T(1,128)} reshape(s32[768]{0:T(1024)} %param.21) | data formatting | bytes 6144 | tf_op jit(solution)/shard_map/reshape | solution.py:575
  11.9 1.9 %plan.1 = (s32[128,128]{1,0:T(8,128)}, s32[1,768]{1,0:T(1,128)}, bf16[256,256]{1,0:T(8,128)(2,1)}, bf16[256,128]{1,0:T(8,128)(2,1)}) custom-call(s32[1,768]{1,0:T(1,128)} %bitcast.19, s32[1,768]{1,0:T(1,128)} %reshape.34.item_ref, s32[1,768]{1,0:T(1,128)} %reshape.35.request_ref, s32[4,32]{1,0:T(4,128)} %probes_ref.1, bf16[64,64]{1,0:T(8,128)(2,1)} %gate_ref.1, ...), custom_call_target="tpu_custom_call" | custom-call | tf_op jit(solution)/shard_map/plan/pallas_call | solution.py:117
  13.8 6.1 %all-to-all-done = bf16[32,32,128]{2,1,0:T(8,128)(2,1)S(1)} async-done(((bf16[32,32,128]{2,1,0:T(8,128)(2,1)}), bf16[32,32,128]{2,1,0:T(8,128)(2,1)S(1)}, u32[]{:S(2)}, u32[]{:S(2)}) %all-to-all-start) | async-done | bytes 262176 | tf_op jit(solution)/shard_map/all_to_all | solution.py:561
  20.0 0.0 copy-start
  20.0 2.6 %all-to-all-start.1 = ((s32[32,4,128]{2,1,0:T(4,128)}), s32[32,4,128]{2,1,0:T(4,128)S(1)}, u32[]{:S(2)}, u32[]{:S(2)}) async-start(s32[32,4,128]{2,1,0:T(4,128)} %bitcast.18), calls=%async_computation.1 | async-start | bytes 131072 | tf_op jit(solution)/shard_map/all_to_all | solution.py:561
  22.5 0.0 copy-done
  22.5 21.3 %score.1.scores_ref = f32[1024,128]{1,0:T(8,128)} custom-call(bf16[1024,128]{1,0:T(8,128)(2,1)} %bitcast.13, bf16[1024,1024]{1,0:T(8,128)(2,1)} %items_hbm.1, bf16[256,256]{1,0:T(8,128)(2,1)} %get-tuple-element.10.gate_ref, bf16[256,128]{1,0:T(8,128)(2,1)} %get-tuple-element.11.bias_ref), custom_call_target="tpu_custom_call" | custom-call | tf_op jit(solution)/shard_map/score/pallas_call | solution.py:206
  43.8 0.0 all-to-all-done.1
  43.8 0.0 copy-start.1
  43.8 0.6 copy-done.1
  44.5 21.0 %rank.1 = f32[128,128]{1,0:T(8,128)} custom-call(f32[1024,128]{1,0:T(8,128)} %score.1.scores_ref, bf16[1024,128]{1,0:T(8,128)(2,1)} %bitcast.14, s32[128,128]{1,0:T(8,128)} %bitcast.15, bf16[1024,1024]{1,0:T(8,128)(2,1)} %items_hbm.1, bf16[3,1024,1024]{2,1,0:T(8,128)(2,1)} %weight_hbm.1, f32[3,1024]{1,0:T(4,128)} %bias_ref.1, f32[1,1024]{1,0:T(1,128)} %bitcast.22), custom_call_target="tpu_custom_call" | custom-call | tf_op jit(solution)/shard_map/rank/pallas_call | solution.py:465
  65.5 13.4 %all_to_all.27 = f32[32,4,128]{2,1,0:T(4,128)} all-to-all(f32[32,4,128]{2,1,0:T(4,128)} %bitcast.16), channel_id=1, replica_groups=mesh['groups'=1,'cand'=32] {'cand'}, dimensions={0} | all-to-all | bytes 131072 | tf_op jit(solution)/shard_map/all_to_all | solution.py:561
  78.8 2.2 %merge.1 = (f32[4,96]{1,0:T(4,128)}, f32[768]{0:T(1024)}) custom-call(f32[128,128]{1,0:T(8,128)} %bitcast.17, s32[1,768]{1,0:T(1,128)} %bitcast.20, s32[1,768]{1,0:T(1,128)} %get-tuple-element.13.place_ref), custom_call_target="tpu_custom_call" | custom-call | tf_op jit(solution)/shard_map/merge/pallas_call | solution.py:546
Async XLA Ops:
  2.1 17.9 %all-to-all-start = ((bf16[32,32,128]{2,1,0:T(8,128)(2,1)}), bf16[32,32,128]{2,1,0:T(8,128)(2,1)S(1)}, u32[]{:S(2)}, u32[]{:S(2)}) async-start(bf16[32,32,128]{2,1,0:T(8,128)(2,1)} %broadcast_in_dim.8), calls=%async_computation | async-start | bytes 524288 | tf_op jit(solution)/shard_map/all_to_all | solution.py:561
  20.0 2.6 %copy-start = (bf16[32,32,128]{2,1,0:T(8,128)(2,1)}, bf16[32,32,128]{2,1,0:T(8,128)(2,1)S(1)}, u32[]{:S(2)}) copy-start(bf16[32,32,128]{2,1,0:T(8,128)(2,1)S(1)} %all-to-all-done) | copy-start | bytes 786436
  20.0 23.9 %all-to-all-start.1 = ((s32[32,4,128]{2,1,0:T(4,128)}), s32[32,4,128]{2,1,0:T(4,128)S(1)}, u32[]{:S(2)}, u32[]{:S(2)}) async-start(s32[32,4,128]{2,1,0:T(4,128)} %bitcast.18), calls=%async_computation.1 | async-start | bytes 131072 | tf_op jit(solution)/shard_map/all_to_all | solution.py:561
  43.8 0.6 copy-start.1

commit v4 on v3

--- a/solution.py
+++ b/solution.py
@@ -18,7 +18,7 @@
 LANES = 128
 SUBLANES = 4
 BLOCKS = 2
-SORT_AT = 0
+SORT_AT = 2
 COLUMNS = 256
 NEVER = -1e30
 TILE_COLS = 256

time: 81.6 us -> 81.5 us (level)
  no operation moved by 1% of the time
where the time goes in v4:
time: 81.5 us; the launch traced here: 81 us
  Pallas kernels  46.4 us (57%)
  blocking collectives  13.4 us (16%)
  starting transfers between devices  9.86 us (12%)
  waiting for transfers between devices  6.13 us (8%)
  local copies, waits for them, and re-layouts  4.62 us (6%)
    pallas_call x1, Pallas kernels, score(): pl.pallas_call(score_kernel, out_shape=jax.ShapeDtypeStruct((item_rows, q...  21.3 us
    pallas_call x1, Pallas kernels, rank(): pl.pallas_call(functools.partial(rank_kernel, fetch=fetch), out_shape=jax...  20.9 us
    all_to_all x1, blocking collectives, exchange(): return lax.all_to_all(x, 'cand', split_axis=0, concat_axis=0, tiled=True)  13.4 us
    all_to_all x2, starting transfers between devices, exchange(): return lax.all_to_all(x, 'cand', split_axis=0, concat_axis=0, tiled=True)  9.86 us
    all_to_all x2, waiting for transfers between devices, exchange(): return lax.all_to_all(x, 'cand', split_axis=0, concat_axis=0, tiled=True)  6.13 us
    pallas_call x1, Pallas kernels, merge(): pl.pallas_call(merge_kernel, out_shape=(jax.ShapeDtypeStruct((local, KEEP...  2.2 us
    pallas_call x1, Pallas kernels, plan(): pl.pallas_call(plan_kernel, out_shape=(jax.ShapeDtypeStruct((size * SUBLA...  1.92 us
  transfers between devices with their start and end apart: 2, of which 1 were waited for; matrix products, arithmetic and copies ran while one was open for 3% of the time, Pallas kernels for 29%

profile of v4, /device:TPU:0, one launch (start us, length us, event | category | flops | bytes accessed | tf_op | source)
XLA Modules:
  0.0 81.0 jit_solution(5107930535028280069)
XLA Ops:
  0.6 1.4 %broadcast_in_dim.8 = bf16[32,32,128]{2,1,0:T(8,128)(2,1)} broadcast(bf16[32,128]{1,0:T(8,128)(2,1)} %bitcast.21), dimensions={1,2} | broadcast | bytes 270336 | tf_op jit(solution)/shard_map/broadcast_in_dim | solution.py:571
  2.1 7.3 %all-to-all-start = ((bf16[32,32,128]{2,1,0:T(8,128)(2,1)}), bf16[32,32,128]{2,1,0:T(8,128)(2,1)S(1)}, u32[]{:S(2)}, u32[]{:S(2)}) async-start(bf16[32,32,128]{2,1,0:T(8,128)(2,1)} %broadcast_in_dim.8), calls=%async_computation | async-start | bytes 524288 | tf_op jit(solution)/shard_map/all_to_all | solution.py:561
  9.4 1.3 %reshape.34.item_ref = s32[1,768]{1,0:T(1,128)} reshape(s32[768]{0:T(1024)} %param.20) | data formatting | bytes 6144 | tf_op jit(solution)/shard_map/reshape | solution.py:575
  10.6 1.3 %reshape.35.request_ref = s32[1,768]{1,0:T(1,128)} reshape(s32[768]{0:T(1024)} %param.21) | data formatting | bytes 6144 | tf_op jit(solution)/shard_map/reshape | solution.py:575
  11.9 1.9 %plan.1 = (s32[128,128]{1,0:T(8,128)}, s32[1,768]{1,0:T(1,128)}, bf16[256,256]{1,0:T(8,128)(2,1)}, bf16[256,128]{1,0:T(8,128)(2,1)}) custom-call(s32[1,768]{1,0:T(1,128)} %bitcast.19, s32[1,768]{1,0:T(1,128)} %reshape.34.item_ref, s32[1,768]{1,0:T(1,128)} %reshape.35.request_ref, s32[4,32]{1,0:T(4,128)} %probes_ref.1, bf16[64,64]{1,0:T(8,128)(2,1)} %gate_ref.1, ...), custom_call_target="tpu_custom_call" | custom-call | tf_op jit(solution)/shard_map/plan/pallas_call | solution.py:117
  13.8 6.1 %all-to-all-done = bf16[32,32,128]{2,1,0:T(8,128)(2,1)S(1)} async-done(((bf16[32,32,128]{2,1,0:T(8,128)(2,1)}), bf16[32,32,128]{2,1,0:T(8,128)(2,1)S(1)}, u32[]{:S(2)}, u32[]{:S(2)}) %all-to-all-start) | async-done | bytes 262176 | tf_op jit(solution)/shard_map/all_to_all | solution.py:561
  20.0 0.0 copy-start
  20.0 2.6 %all-to-all-start.1 = ((s32[32,4,128]{2,1,0:T(4,128)}), s32[32,4,128]{2,1,0:T(4,128)S(1)}, u32[]{:S(2)}, u32[]{:S(2)}) async-start(s32[32,4,128]{2,1,0:T(4,128)} %bitcast.18), calls=%async_computation.1 | async-start | bytes 131072 | tf_op jit(solution)/shard_map/all_to_all | solution.py:561
  22.5 0.0 copy-done
  22.5 21.3 %score.1.scores_ref = f32[1024,128]{1,0:T(8,128)} custom-call(bf16[1024,128]{1,0:T(8,128)(2,1)} %bitcast.13, bf16[1024,1024]{1,0:T(8,128)(2,1)} %items_hbm.1, bf16[256,256]{1,0:T(8,128)(2,1)} %get-tuple-element.10.gate_ref, bf16[256,128]{1,0:T(8,128)(2,1)} %get-tuple-element.11.bias_ref), custom_call_target="tpu_custom_call" | custom-call | tf_op jit(solution)/shard_map/score/pallas_call | solution.py:206
  43.8 0.0 all-to-all-done.1
  43.8 0.0 copy-start.1
  43.8 0.6 copy-done.1
  44.5 20.9 %rank.1 = f32[128,128]{1,0:T(8,128)} custom-call(f32[1024,128]{1,0:T(8,128)} %score.1.scores_ref, bf16[1024,128]{1,0:T(8,128)(2,1)} %bitcast.14, s32[128,128]{1,0:T(8,128)} %bitcast.15, bf16[1024,1024]{1,0:T(8,128)(2,1)} %items_hbm.1, bf16[3,1024,1024]{2,1,0:T(8,128)(2,1)} %weight_hbm.1, f32[3,1024]{1,0:T(4,128)} %bias_ref.1, f32[1,1024]{1,0:T(1,128)} %bitcast.22), custom_call_target="tpu_custom_call" | custom-call | tf_op jit(solution)/shard_map/rank/pallas_call | solution.py:465
  65.4 13.4 %all_to_all.27 = f32[32,4,128]{2,1,0:T(4,128)} all-to-all(f32[32,4,128]{2,1,0:T(4,128)} %bitcast.16), channel_id=1, replica_groups=mesh['groups'=1,'cand'=32] {'cand'}, dimensions={0} | all-to-all | bytes 131072 | tf_op jit(solution)/shard_map/all_to_all | solution.py:561
  78.8 2.2 %merge.1 = (f32[4,96]{1,0:T(4,128)}, f32[768]{0:T(1024)}) custom-call(f32[128,128]{1,0:T(8,128)} %bitcast.17, s32[1,768]{1,0:T(1,128)} %bitcast.20, s32[1,768]{1,0:T(1,128)} %get-tuple-element.13.place_ref), custom_call_target="tpu_custom_call" | custom-call | tf_op jit(solution)/shard_map/merge/pallas_call | solution.py:546
Async XLA Ops:
  2.1 17.9 %all-to-all-start = ((bf16[32,32,128]{2,1,0:T(8,128)(2,1)}), bf16[32,32,128]{2,1,0:T(8,128)(2,1)S(1)}, u32[]{:S(2)}, u32[]{:S(2)}) async-start(bf16[32,32,128]{2,1,0:T(8,128)(2,1)} %broadcast_in_dim.8), calls=%async_computation | async-start | bytes 524288 | tf_op jit(solution)/shard_map/all_to_all | solution.py:561
  20.0 2.6 %copy-start = (bf16[32,32,128]{2,1,0:T(8,128)(2,1)}, bf16[32,32,128]{2,1,0:T(8,128)(2,1)S(1)}, u32[]{:S(2)}) copy-start(bf16[32,32,128]{2,1,0:T(8,128)(2,1)S(1)} %all-to-all-done) | copy-start | bytes 786436
  20.0 23.9 %all-to-all-start.1 = ((s32[32,4,128]{2,1,0:T(4,128)}), s32[32,4,128]{2,1,0:T(4,128)S(1)}, u32[]{:S(2)}, u32[]{:S(2)}) async-start(s32[32,4,128]{2,1,0:T(4,128)} %bitcast.18), calls=%async_computation.1 | async-start | bytes 131072 | tf_op jit(solution)/shard_map/all_to_all | solution.py:561
  43.8 0.6 copy-start.1
